TPU v7x, 32 devices: a whole 2x2x4 slice. The times are simulated.
32 devices in a mesh: group: 2 (over y), seq: 16 (over z, x, core).
Axes of the slice: x: 2, y: 2, z: 4, core: 2. Of those that a mesh axis runs over, the one named last changes fastest.
Arguments:
- prompt_raw: bfloat16 [32, 512, 576], P(('group', 'seq')), parts along dimension 0, may hold values from -6 to 6
- lengths: int32 [32], P('group'), parts along dimension 0, may hold values from 1 to 512, 6144 in all
- owners: int32 [32], P('group'), parts along dimension 0, may hold values from 0 to 15, as said below
- resident: bfloat16 [64, 1024, 576], P(('group', 'seq')), parts along dimension 0, may hold values from -6 to 6
- new_raw: bfloat16 [32, 2, 576], P('group'), parts along dimension 0, may hold values from -6 to 6
- queries: bfloat16 [32, 2, 16, 192], P('group', None, 'seq'), parts along dimension 0, may hold values from -100 to 100
- kv_gain: bfloat16 [512], replicated, may hold values from 0.099609375 to 1.8984375
- w_uk: bfloat16 [16, 128, 512], P('seq'), may hold values from -0.5 to 0.5
- w_uv: bfloat16 [16, 512, 128], P('seq'), may hold values from -3 to 3
- w_o: bfloat16 [16, 128, 7168], P('seq'), may hold values from -0.125 to 0.125
Outputs:
- layer_out: bfloat16 [32, 2, 7168], P(('group', 'seq')), parts along dimension 0
There are 2 independent parts, one for each index of `group`. A program takes and returns all parts, laid end to end along the dimension named above; an argument that names none is the same for every part. Nothing has to cross between parts.
Inputs may be any that keep to these rules, and one draw needn't show every extreme that they name: `owners`: no device is the owner of more than 2 sequences, and some device owns exactly 2.
All inputs are finite; a program needn't handle non-finite values.
Results may differ from a plain program's by a relative error of at most 0.0096.
Values may be sent and summed in bfloat16 or wider, within the bound.
No kernel may reach another device: no remote copies, remote signals or barrier semaphores. Data moves between devices by JAX's collectives and lax.ppermute only.
A program may use at most 64 MiB of HBM per device.

v0:
```python
import functools

import jax
import jax.numpy as jnp
import numpy as np
from jax import lax
from jax.experimental import pallas as pl
from jax.experimental.pallas import tpu as pltpu
from jax.sharding import PartitionSpec as P

F32 = jnp.float32
BF16 = jnp.bfloat16
I32 = jnp.int32
I16 = jnp.int16
VMEM = pl.BlockSpec(memory_space=pltpu.VMEM)
SMEM = pl.BlockSpec(memory_space=pltpu.SMEM)
HBM = pl.BlockSpec(memory_space=pltpu.HBM)
LANES = 128
PACK = 16
PART = 6
BITS = 14.0
NEAR = 4


def iota(shape, dim):
    return lax.broadcasted_iota(I32, shape, dim)


def shift_of(count):
    return count // 2 + 2


def over(x, n):
    return x >> (n.bit_length() - 1)


def rest_of(x, n):
    return x & (n - 1)


def dot(a, b, dims=((1,), (0,))):
    return lax.dot_general(a, b, (dims, ((), ())), preferred_element_type=F32)


def column_of(row, picks):
    n, width = picks.shape[0], row.shape[1]
    hit = iota((n, width), 1) == picks
    return jnp.sum(jnp.where(hit, row, 0), axis=1, keepdims=True)


def slots_of(owners_row):
    seqs = owners_row.shape[1]
    owners_col = column_of(owners_row, iota((seqs, 1), 0))
    earlier = iota((seqs, seqs), 0) < iota((seqs, seqs), 1)
    same = (owners_col == owners_row) & earlier
    return jnp.sum(jnp.where(same, 1, 0), axis=0, keepdims=True)


def doubled(row, times):
    seqs = row.shape[1]
    col = column_of(row, iota((seqs, 1), 0))
    shape = (seqs, 2 * seqs * times)
    hit = over(rest_of(iota(shape, 1), 2 * seqs), 2) == iota(shape, 0)
    return jnp.sum(jnp.where(hit, col, 0), axis=0, keepdims=True)


def frequencies(half, shape, dim):
    at = rest_of(iota(shape, dim), half)
    values = np.float32(10000.0) ** (-(np.arange(half, dtype=np.float32) * np.float32(2.0)) / np.float32(2 * half))
    result = jnp.zeros(shape, F32)
    for i in range(half):
        result = jnp.where(at == i, float(values[i]), result)
    return result


def sine_cosine(angle):
    count = jnp.floor(angle * (2.0 / np.pi) + 0.5)
    x = ((angle - count * 1.5703125) - count * 4.837512969970703125e-4) - count * 7.54978995489188216e-8
    quarter = count.astype(I32)
    y = x * x
    sine = x + x * y * (-1.6666654611e-1 + y * (8.3321608736e-3 - y * 1.9515295891e-4))
    cosine = 1.0 - 0.5 * y + y * y * (4.166664568298827e-2 + y * (-1.388731625493765e-3 + y * 2.443315711809948e-5))
    odd = rest_of(quarter, 2) == 1
    first, second = jnp.where(odd, cosine, sine), jnp.where(odd, sine, cosine)
    first = jnp.where(rest_of(quarter, 4) >= 2, -first, first)
    second = jnp.where(rest_of(quarter + 1, 4) >= 2, -second, second)
    return first, second


def query_kernel(
    res_rows,
    owners_hbm,
    lengths_hbm,
    queries_hbm,
    uk_hbm,
    new_hbm,
    gain_hbm,
    out_ref,
    aux_ref,
    owners_ref,
    lengths_ref,
    queries_ref,
    uk_ref,
    new_ref,
    gain_ref,
    flat,
    sems,
):
    device = lax.axis_index("seq")
    copies = []
    pairs = [
        (owners_hbm, owners_ref),
        (lengths_hbm, lengths_ref),
        (queries_hbm, queries_ref),
        (uk_hbm, uk_ref),
        (new_hbm.at[device], new_ref),
        (gain_hbm, gain_ref),
    ]
    for n, (source, target) in enumerate(pairs):
        copies.append(pltpu.make_async_copy(source, target, sems.at[n]))
        copies[-1].start()
    for copy in copies:
        copy.wait()
    seqs = owners_ref.shape[1]
    nope, latent = uk_ref.shape
    rope = queries_ref.shape[3] - nope
    half = latent // 2
    rows = 2 * seqs
    for s in range(seqs):
        flat[2 * s : 2 * s + 2, : nope + rope] = queries_ref[s, 0].astype(F32)
    values = flat[:, : nope + rope]
    absorbed = dot(values[:, :nope].astype(BF16), uk_ref[...]).astype(BF16)
    row = iota((rows, 1), 0)
    lengths = column_of(lengths_ref[...], over(row, 2))
    angle = (res_rows + lengths + rest_of(row, 2)).astype(F32) * frequencies(rope // 2, (1, rope), 1)
    x = values[:, nope:]
    swapped = jnp.concatenate([x[:, rope // 2 :], x[:, : rope // 2]], axis=1)
    sine, cosine = sine_cosine(angle)
    sine = jnp.where(iota(x.shape, 1) < rope // 2, -sine, sine)
    turned = x * cosine + swapped * sine
    zero = jnp.zeros((rows, rope), F32)
    pieces = [absorbed[:, :half], absorbed[:, half:]]
    for k in range(3):
        blocks = [turned if j == k else zero for j in range(half // rope)]
        pieces.append(jnp.concatenate(blocks, axis=1).astype(BF16))
    owners = owners_ref[...]
    owner = doubled(owners, 5)
    slot = doubled(slots_of(owners), 5)
    shape = (out_ref.shape[0] * PACK, 5 * rows)
    dest, r = over(iota(shape, 0), PACK) ^ shift_of(out_ref.shape[0]), rest_of(iota(shape, 0), PACK)
    lane = iota((1, 5 * rows), 1)
    piece, seq, tok = over(lane, rows), over(rest_of(lane, rows), 2), rest_of(lane, 2)
    start = jnp.where(piece < 2, piece * PART, 2 * PART) + tok
    offset = r - start
    rotary = piece >= 2
    third = piece - 2
    here = jnp.where(owner == dest, slot + 1, jnp.where(seq == dest, 0, -1))
    both = (owner == dest) & (seq == dest)
    wide = (offset == 2 * here) | (both & (offset == 0))
    narrow = (offset == 0) & ((here == third) | (both & (third == 0)))
    hit = (~rotary & (here >= 0) & wide) | (rotary & narrow)
    pieces = jnp.concatenate(pieces, axis=0)
    result = dot(jnp.where(hit, 1.0, 0.0).astype(BF16), pieces)
    out_ref[...] = result.astype(BF16).reshape(out_ref.shape)
    width = new_ref.shape[1]
    aux_ref[0:2, :width] = new_ref[...].astype(F32)
    mine = jnp.where(iota(lengths_ref.shape, 1) == device, lengths_ref[...], 0)
    mine = jnp.sum(mine, axis=1, keepdims=True).astype(F32)
    aux_ref[2:3, :] = jnp.broadcast_to(mine, (1, aux_ref.shape[1]))
    aux_ref[3:4, :latent] = gain_ref[...].astype(F32).reshape(1, latent)


def fetch_start(source, target, sem, first):
    copy = pltpu.make_async_copy(source.at[:, pl.ds(first, target.shape[1]), :], target, sem)
    copy.start()
    return copy


def compress_kernel(
    res_rows, latent, aux_ref, prompt_ref, resident_hbm, out_ref, bias_ref, resident_ref, sem
):
    fetch = pltpu.make_async_copy(resident_hbm, resident_ref, sem)
    fetch.start()
    width, most = prompt_ref.shape[1:]
    half = (width - latent) // 2
    fresh = jnp.concatenate([aux_ref[0:2, :width], jnp.zeros((PACK - 2, width), F32)], axis=0)
    pick = jnp.where(iota((PACK, LANES), 0) == iota((PACK, LANES), 1), 1.0, 0.0).astype(BF16)
    fresh = dot(fresh.astype(BF16), pick, ((0,), (0,)))
    gain = jnp.broadcast_to(aux_ref[3:4, :latent], (PACK, latent))
    top = jnp.where(iota((PACK, LANES), 0) == 0, 1.0, 0.0).astype(BF16)
    gain = dot(gain.astype(BF16), top, ((0,), (0,)))
    length = aux_ref[2:3, :LANES].astype(I32)
    at = iota(bias_ref.shape, 1)
    token = iota(bias_ref.shape, 0)
    length_all = jnp.concatenate([length] * (bias_ref.shape[1] // LANES), axis=1)
    seen = (at < length_all) | ((at >= most) & (at <= most + token))
    bias_ref[...] = jnp.where(seen, 1.0, 0.0)
    freq = frequencies(half, (half, 1), 0)
    for i in range(most // LANES + 1):
        at = slice(i * LANES, (i + 1) * LANES)
        lane = iota((1, LANES), 1)
        if i * LANES < most:
            raw = prompt_ref[0, :, at].astype(F32)
            position = res_rows + i * LANES + lane
        else:
            raw = fresh
            position = res_rows + length + lane
        lat = raw[:latent]
        meansq = jnp.sum(lat * lat, axis=0, keepdims=True) * (1.0 / latent)
        out_ref[:latent, at] = (lat * lax.rsqrt(meansq + 1e-06) * gain).astype(BF16)
        angle = position.astype(F32) * freq
        sine, cosine = sine_cosine(angle)
        x1, x2 = raw[latent : latent + half], raw[latent + half :]
        out_ref[latent : latent + half, at] = (x1 * cosine - x2 * sine).astype(BF16)
        out_ref[latent + half :, at] = (x2 * cosine + x1 * sine).astype(BF16)
    fetch.wait()


def score_kernel(
    scale, q_ref, keys_ref, seen_ref, resident_ref, wo_hbm, sp_ref, sr_ref, stat_ref, wo_ref, sem
):
    fetch = fetch_start(wo_hbm, wo_ref, sem, 0)
    heads = q_ref.shape[0]
    half = q_ref.shape[2]
    width = keys_ref.shape[0]
    rope = width - 2 * half
    rows = 2 * heads
    total = heads * PACK
    flat = q_ref[...].reshape(total, half)
    shape = (rows, total)
    line = iota(shape, 0)
    head, tok = over(line, 4) * 2 + rest_of(line, 2), rest_of(over(line, 2), 2)
    source = iota(shape, 1) - head * PACK

    def picked(r):
        hit = source == r + tok
        return dot(jnp.where(hit, 1.0, 0.0).astype(BF16), flat)

    turned = picked(2 * PART)
    tops, sums = [], []
    for k in range(3):
        query = jnp.concatenate(
            [picked(2 * k), picked(PART + 2 * k), turned[:, k * rope : (k + 1) * rope]], axis=1
        ).astype(BF16)
        keys = keys_ref[...] if k == 0 else resident_ref[k - 1]
        scores = dot(query, keys) * scale
        if k == 0:
            first, second = seen_ref[0:1, :] > 0.5, seen_ref[1:2, :] > 0.5
            token = rest_of(over(iota(scores.shape, 0), 2), 2)
            seen = (first & (token == 0)) | (second & (token == 1))
            scores = jnp.where(seen, scores, -1e30)
            sp_ref[...] = scores
        else:
            sr_ref[k - 1] = scores
        top = jnp.max(scores, axis=1, keepdims=True)
        tops.append(top)
        sums.append(jnp.sum(jnp.exp(scores - top), axis=1, keepdims=True))
    lanes = stat_ref.shape[2]
    here = iota((3 * rows, lanes), 0) == iota((3 * rows, lanes), 1)
    top = jnp.sum(jnp.where(here, jnp.concatenate(tops, axis=0), 0.0), axis=0, keepdims=True)
    total = jnp.sum(jnp.where(here, jnp.concatenate(sums, axis=0), 0.0), axis=0, keepdims=True)
    both = jnp.concatenate([top, total], axis=0)
    stat_ref[...] = jnp.broadcast_to(both[None], stat_ref.shape)
    fetch.wait()


def attend_kernel(
    owners_ref, stat_ref, sp_ref, sr_ref, keys_ref, resident_ref, wo_hbm, out_ref, wo_ref, sem
):
    fetch = fetch_start(wo_hbm, wo_ref, sem, wo_ref.shape[1])
    heads = out_ref.shape[0]
    latent = out_ref.shape[1] // PART * LANES
    seqs = owners_ref.shape[0]
    rows = 2 * heads
    device = lax.axis_index("seq")
    lanes = stat_ref.shape[2]
    my_owner = owners_ref[device]
    my_slot = jnp.int32(0)
    seen = jnp.int32(0)
    first = jnp.int32(0)
    second = jnp.int32(0)
    for s in range(seqs):
        owner = owners_ref[s]
        my_slot = my_slot + jnp.where((owner == my_owner) & (s < device), 1, 0)
        mine = owner == device
        first = jnp.where(mine & (seen == 0), s, first)
        second = jnp.where(mine & (seen == 1), s, second)
        seen = seen + jnp.where(mine, 1, 0)

    shift = shift_of(heads)
    mine = stat_ref[device ^ shift]
    place = over(iota((1, lanes), 1), rows)
    other = jnp.zeros((2, lanes), F32)
    pairs = [
        (stat_ref[my_owner ^ shift], 1 + my_slot),
        (stat_ref[first ^ shift], 0),
        (stat_ref[second ^ shift], 0),
    ]
    for k, (theirs, segment) in enumerate(pairs):
        moved = jnp.zeros((2, lanes), F32)
        for n in range(3):
            turned = pltpu.roll(theirs, ((k - n) * rows) % lanes, 1)
            moved = jnp.where(segment == n, turned, moved)
        other = jnp.where(place == k, moved, other)
    top = jnp.maximum(mine[0:1], other[0:1])
    total = mine[1:2] * jnp.exp(mine[0:1] - top) + other[1:2] * jnp.exp(other[0:1] - top)
    hit = iota((3 * rows, lanes), 1) == iota((3 * rows, lanes), 0)
    top = jnp.sum(jnp.where(hit, top, 0.0), axis=1, keepdims=True)
    total = jnp.sum(jnp.where(hit, total, 0.0), axis=1, keepdims=True)
    for k in range(3):
        at = slice(k * rows, (k + 1) * rows)
        scores = sp_ref[...] if k == 0 else sr_ref[k - 1]
        keys = keys_ref[:latent, :] if k == 0 else resident_ref[k - 1, :latent, :]
        weights = jnp.exp(scores - top[at]).astype(BF16)
        part = dot(weights, keys, ((1,), (1,))) / total[at]
        for h in range(heads):
            for c in range(latent // LANES):
                at = c * PART + 2 * k
                out_ref[h, at : at + 2, :] = part[2 * h : 2 * h + 2, c * LANES : (c + 1) * LANES]
    fetch.wait()


def project_kernel(
    owners_ref, part_ref, uv_ref, other_uv_ref, wo_ref, other_wo0_ref, other_wo1_ref, out_ref
):
    count, each, lanes = part_ref.shape
    seqs = owners_ref.shape[1]
    cuts = each // PART
    rows = 2 * seqs
    core = lax.axis_index("seq") % 2
    owners = owners_ref[...]
    row = iota((cuts * 2 * rows, 1), 0)
    cut, other, seq = over(row, 2 * rows), over(rest_of(row, 2 * rows), rows), over(rest_of(row, rows), 2)
    shift = shift_of(count)
    seq = seq ^ shift
    head = jnp.where(other == 0, core, 1 - core)
    owner = column_of(owners, seq)
    slot = column_of(slots_of(owners), seq)
    first = (seq ^ shift) * each + cut * PART + head
    second = (owner ^ shift) * each + cut * PART + 2 + 2 * slot + head
    at = iota((cuts * 2 * rows, count * each), 1)
    hit = jnp.where((at == first) | (at == second), 1.0, 0.0).astype(BF16)
    rest = part_ref[...].reshape(count * each, lanes)
    latent = None
    for _ in range(3):
        piece = rest.astype(BF16)
        rest = rest - piece.astype(F32)
        one = dot(hit, piece)
        latent = one if latent is None else latent + one
    latent = latent.astype(BF16)
    latent = jnp.concatenate(
        [latent[c * 2 * rows : (c + 1) * 2 * rows] for c in range(cuts)], axis=1
    )
    half = rest_of(iota((rows, 1), 0), 2)
    cols = wo_ref.shape[2] // 2
    product = None
    depth = other_wo0_ref.shape[1]
    for n, uv in enumerate((uv_ref, other_uv_ref)):
        head_out = dot(latent[n * rows : (n + 1) * rows], uv[0])
        weights = [wo_ref] if n == 0 else [other_wo0_ref, other_wo1_ref]
        for side in range(2):
            lines = jnp.where(half == side, head_out, 0.0).astype(BF16)
            for i, wo in enumerate(weights):
                line = lines if n == 0 else lines[:, i * depth : (i + 1) * depth]
                one = dot(line, wo[0, :, side * cols : (side + 1) * cols])
                product = one if product is None else product + one
    top = jnp.max(jnp.abs(product), axis=1, keepdims=True)
    power = jnp.clip(jnp.floor(jnp.log2(jnp.maximum(top, 1e-35))) + 1.0, -100.0, 100.0)
    coded = jnp.round(product * jnp.exp2(BITS - power)).astype(I32).astype(I16)
    power = jnp.broadcast_to(power, (rows, LANES)).astype(I32).astype(I16)
    for s in range(seqs):
        out_ref[s, :, :cols] = coded[2 * s : 2 * s + 2]
        out_ref[s, :, cols:] = power[2 * s : 2 * s + 2]


def final_kernel(in_ref, out_ref):
    cols = out_ref.shape[2] // 2
    for t in range(2):
        total = None
        for n in range(t, in_ref.shape[0], 2):
            power = in_ref[n, :, cols : cols + 1].astype(I32).astype(F32)
            one = in_ref[n, :, :cols].astype(I32).astype(F32) * jnp.exp2(power - BITS)
            total = one if total is None else total + one
        for j in range(2):
            out_ref[0, t : t + 1, j * cols : (j + 1) * cols] = total[j : j + 1].astype(BF16)


def swap(x):
    count = lax.axis_size("seq")
    order = [p ^ shift_of(count) for p in range(count)]
    return lax.all_to_all(x, "seq", split_axis=0, concat_axis=0, axis_index_groups=[order], tiled=True)


def trade(x, step):
    count = lax.axis_size("seq")
    return lax.ppermute(x, "seq", [(d, d ^ step) for d in range(count)])


def call(kernel, shapes, specs, scratch=(), cost=None, room=None):
    single = not isinstance(shapes, (list, tuple))
    if room is None:
        room = 16 if lax.axis_size("seq") <= 32 else 56
    return pl.pallas_call(
        kernel,
        out_shape=shapes,
        in_specs=specs,
        out_specs=VMEM if single else [VMEM] * len(shapes),
        scratch_shapes=list(scratch),
        cost_estimate=cost,
        compiler_params=pltpu.CompilerParams(vmem_limit_bytes=room * 1024 * 1024),
    )


def on_device(prompt_raw, lengths, owners, resident, new_raw, queries, kv_gain, w_uk, w_uv, w_o):
    count = lax.axis_size("seq")
    seqs = lengths.shape[0]
    most, width = prompt_raw.shape[1:]
    latent = kv_gain.shape[0]
    res_rows = resident.shape[1]
    nope = w_uk.shape[1]
    rope = width - latent
    heads = count
    out_width = w_o.shape[2]
    scale = 1.0 / queries.shape[-1] ** 0.5
    owners_row, lengths_row = owners.reshape(1, seqs), lengths.reshape(1, seqs)
    prompt_raw = prompt_raw.transpose(0, 2, 1)
    resident = resident.transpose(0, 2, 1)
    queries = queries.transpose(0, 2, 1, 3)
    keys_rows = most + LANES

    aux_width = -(-width // LANES) * LANES
    query, aux = call(
        functools.partial(query_kernel, res_rows),
        [
            jax.ShapeDtypeStruct((count, PACK, latent // 2), BF16),
            jax.ShapeDtypeStruct((8, aux_width), F32),
        ],
        [HBM] * 6,
        [
            pltpu.VMEM((1, seqs), I32),
            pltpu.VMEM((1, seqs), I32),
            pltpu.VMEM(queries.shape, BF16),
            pltpu.VMEM((nope, latent), BF16),
            pltpu.VMEM((2, width), BF16),
            pltpu.VMEM((latent,), BF16),
            pltpu.VMEM((2 * seqs, -(-(nope + rope) // LANES) * LANES), F32),
            pltpu.SemaphoreType.DMA((6,)),
        ],
        room=60,
    )(owners_row, lengths_row, queries, w_uk[0], new_raw, kv_gain)
    received = swap(query)
    query, w_uv, w_o = lax.optimization_barrier((query, w_uv, w_o))
    other_uv, other_wo = trade(w_uv, 1), trade(w_o, 1)
    keys, seen, resident = call(
        functools.partial(compress_kernel, res_rows, latent),
        [
            jax.ShapeDtypeStruct((width, keys_rows), BF16),
            jax.ShapeDtypeStruct((8, keys_rows), F32),
            jax.ShapeDtypeStruct(resident.shape, BF16),
        ],
        [VMEM] * 2 + [HBM],
        [pltpu.SemaphoreType.DMA],
        cost=pl.CostEstimate(flops=10**7, bytes_accessed=10**7, transcendentals=10**5),
    )(aux, prompt_raw, resident)
    lanes = -(-6 * heads // LANES) * LANES
    half = out_width // 2
    half_wo = jax.ShapeDtypeStruct((1, w_o.shape[1] // 2, out_width), BF16)
    scores_p, scores_r, stat, other_wo0 = call(
        functools.partial(score_kernel, scale),
        [
            jax.ShapeDtypeStruct((2 * heads, keys_rows), F32),
            jax.ShapeDtypeStruct((2, 2 * heads, res_rows), F32),
            jax.ShapeDtypeStruct((count, 2, lanes), F32),
            half_wo,
        ],
        [VMEM] * 4 + [HBM],
        [pltpu.SemaphoreType.DMA],
    )(received, keys, seen, resident, other_wo)
    stat, other_uv = lax.optimization_barrier((stat, other_uv))
    stats = swap(stat)
    part, other_wo1 = call(
        attend_kernel,
        [
            jax.ShapeDtypeStruct((heads, PART * (latent // LANES), LANES), F32),
            half_wo,
        ],
        [SMEM] + [VMEM] * 5 + [HBM],
        [pltpu.SemaphoreType.DMA],
    )(owners, stats, scores_p, scores_r, keys, resident, other_wo)
    parts = swap(part)
    sums = call(
        project_kernel, jax.ShapeDtypeStruct((seqs, 2, half + LANES), I16), [VMEM] * 7
    )(owners_row, parts, w_uv, other_uv, w_o, other_wo0, other_wo1)
    return call(final_kernel, jax.ShapeDtypeStruct((1, 2, out_width), BF16), [VMEM])(swap(sums))


def solution(mesh):
    in_specs = (
        P(("group", "seq"), None, None),
        P("group"),
        P("group"),
        P(("group", "seq"), None, None),
        P("group", None, None),
        P("group", None, "seq", None),
        P(),
        P("seq", None, None),
        P("seq", None, None),
        P("seq", None, None),
    )
    out_specs = P(("group", "seq"), None, None)
    return jax.shard_map(
        on_device, mesh=mesh, in_specs=in_specs, out_specs=out_specs, check_vma=False
    )
```

profile of v0, /device:TPU:1, one launch (start us, length us, event | category | flops | bytes accessed | tf_op | source)
XLA Modules:
  0.0 51.0 jit_solution(11668248616474373702)
XLA Ops:
  0.0 2.3 %shard_map.100 = (bf16[16,16,256]{2,1,0:T(8,128)(2,1)}, f32[8,640]{1,0:T(8,128)}) custom-call(s32[1,16]{1,0:T(1,128)} %bitcast.8, s32[1,16]{1,0:T(1,128)} %bitcast.12, bf16[16,1,2,192]{3,2,1,0:T(2,128)(2,1)} %bitcast.11, bf16[128,512]{1,0:T(8,128)(2,1)} %bitcast.10, bf16[16,2,576]{2,1,0:T(2,128)(2,1)} %new_hbm.1, bf16[512]{0:T(512)(128)(2,1)} %gain_hbm.1), custom_call_target="tpu_custom_call" | custom-call | tf_op jit(solution)/shard_map/pallas_call | solution.py:432
  2.3 0.1 collective-permute-start
  2.5 8.0 %all-to-all-start = ((bf16[16,16,256]{2,1,0:T(8,128)(2,1)}), bf16[16,16,256]{2,1,0:T(8,128)(2,1)S(1)}, u32[]{:S(2)}, u32[]{:S(2)}) async-start(bf16[16,16,256]{2,1,0:T(8,128)(2,1)} %get-tuple-element.20), calls=%async_computation | async-start | bytes 262144 | tf_op jit(solution)/shard_map/all_to_all | solution.py:391
  10.4 0.4 collective-permute-start.1
  10.8 0.0 copy-start
  10.8 1.7 %copy-done = bf16[2,1024,576]{1,2,0:T(8,128)(2,1)S(1)} copy-done((bf16[2,1024,576]{1,2,0:T(8,128)(2,1)S(1)}, bf16[2,1024,576]{1,2,0:T(8,128)(2,1)}, u32[]{:S(2)}) %copy-start) | copy-done | bytes 2359320
  12.5 0.0 copy-start.2
  12.5 1.1 %copy-done.2 = bf16[1,512,576]{1,2,0:T(8,128)(2,1)S(1)} copy-done((bf16[1,512,576]{1,2,0:T(8,128)(2,1)S(1)}, bf16[1,512,576]{1,2,0:T(8,128)(2,1)}, u32[]{:S(2)}) %copy-start.2) | copy-done | bytes 589848
  13.5 0.0 copy-start.4
  13.5 0.7 %copy-done.4 = f32[8,640]{1,0:T(8,128)S(1)} copy-done((f32[8,640]{1,0:T(8,128)S(1)}, f32[8,640]{1,0:T(8,128)}, u32[]{:S(2)}) %copy-start.4) | copy-done | bytes 20504
  14.3 0.8 %shard_map.101 = (bf16[576,640]{1,0:T(8,128)(2,1)S(1)}, f32[8,640]{1,0:T(8,128)S(1)}, bf16[2,576,1024]{2,1,0:T(8,128)(2,1)S(1)}) custom-call(f32[8,640]{1,0:T(8,128)S(1)} %copy-done.4, bf16[1,576,512]{2,1,0:T(8,128)(2,1)S(1)} %bitcast.7, bf16[2,576,1024]{2,1,0:T(8,128)(2,1)S(1)} %bitcast.6), custom_call_target="tpu_custom_call" | custom-call | flops 10000000 | bytes 10000000 | tf_op jit(solution)/shard_map/pallas_call | solution.py:454
  15.0 0.0 all-to-all-done.q_ref
  15.0 0.0 collective-permute-done.wo_hbm
  15.1 0.0 copy-start.5
  15.1 1.4 %shard_map.102 = (f32[32,640]{1,0:T(8,128)S(1)}, f32[2,32,1024]{2,1,0:T(8,128)S(1)}, f32[16,2,128]{2,1,0:T(2,128)S(1)}, bf16[1,64,7168]{2,1,0:T(8,128)(2,1)S(1)}) custom-call(bf16[16,16,256]{2,1,0:T(8,128)(2,1)S(1)} %all-to-all-done.q_ref, bf16[576,640]{1,0:T(8,128)(2,1)S(1)} %get-tuple-element.22.keys_ref, f32[8,640]{1,0:T(8,128)S(1)} %get-tuple-element.23.seen_ref, ...), custom_call_target="tpu_custom_call" | custom-call | tf_op jit(solution)/shard_map/pallas_call | solution.py:468
  16.5 0.0 collective-permute-done.1.other_uv_ref
  16.5 8.2 %all_to_all.20.stat_ref = f32[16,2,128]{2,1,0:T(2,128)S(1)} all-to-all(f32[16,2,128]{2,1,0:T(2,128)S(1)} %get-tuple-element.28), channel_id=1, replica_groups={{10,11,8,9,14,15,12,13,2,3,0,1,6,7,4,5},{26,27,24,25,30,31,28,29,18,19,..., dimensions={0} | all-to-all | bytes 32768 | tf_op jit(solution)/shard_map/all_to_all | solution.py:391
  24.8 0.0 copy-done.5
  24.8 0.0 copy-start.1
  24.8 0.0 copy-start.3
  24.8 1.8 %shard_map.103 = (f32[16,24,128]{2,1,0:T(8,128)S(1)}, bf16[1,64,7168]{2,1,0:T(8,128)(2,1)S(1)}) custom-call(s32[16]{0:T(128)S(1)} %copy-done.5, f32[16,2,128]{2,1,0:T(2,128)S(1)} %all_to_all.20.stat_ref, f32[32,640]{1,0:T(8,128)S(1)} %get-tuple-element.29.sp_ref, f32[2,32,1024]{2,1,0:T(8,128)S(1)} %get-tuple-element.30.sr_ref, ...), custom_call_target="tpu_custom_call" | custom-call | tf_op jit(solution)/shard_map/pallas_call | solution.py:481
  26.6 10.3 %all_to_all.21.part_ref = f32[16,24,128]{2,1,0:T(8,128)S(1)} all-to-all(f32[16,24,128]{2,1,0:T(8,128)S(1)} %get-tuple-element.31), channel_id=1, replica_groups={{10,11,8,9,14,15,12,13,2,3,0,1,6,7,4,5},{26,27,24,25,30,31,28,29,18,19,..., dimensions={0} | all-to-all | bytes 393216 | tf_op jit(solution)/shard_map/all_to_all | solution.py:391
  36.9 0.0 copy-done.1
  36.9 0.0 copy-done.3
  36.9 1.6 %shard_map.104 = s16[16,2,3712]{2,1,0:T(2,128)(2,1)S(1)} custom-call(s32[1,16]{1,0:T(1,128)S(1)} %bitcast.9, f32[16,24,128]{2,1,0:T(8,128)S(1)} %all_to_all.21.part_ref, bf16[1,512,128]{2,1,0:T(8,128)(2,1)S(1)} %copy-done.3, bf16[1,512,128]{2,1,0:T(8,128)(2,1)S(1)} %collective-permute-done.1.other_uv_ref, bf16[1,128,7168]{2,1,0:T(8,128)(2,1)S(1)} %copy-done.1, ...), custom_call_target="tpu_custom_call" | custom-call | tf_op jit(solution)/shard_map/pallas_call | solution.py:491
  38.5 11.7 %all_to_all.22.in_ref = s16[16,2,3712]{2,1,0:T(2,128)(2,1)S(1)} all-to-all(s16[16,2,3712]{2,1,0:T(2,128)(2,1)S(1)} %shard_map.104), channel_id=1, replica_groups={{10,11,8,9,14,15,12,13,2,3,0,1,6,7,4,5},{26,27,24,25,30,31,28,29,18,19,..., dimensions={0} | all-to-all | bytes 475136 | tf_op jit(solution)/shard_map/all_to_all | solution.py:391
  50.2 0.8 %shard_map.105 = bf16[1,2,7168]{2,1,0:T(2,128)(2,1)} custom-call(s16[16,2,3712]{2,1,0:T(2,128)(2,1)S(1)} %all_to_all.22.in_ref), custom_call_target="tpu_custom_call" | custom-call | tf_op jit(solution)/shard_map/pallas_call | solution.py:494
Async XLA Ops:
  2.3 12.7 %collective-permute-start = (bf16[1,128,7168]{2,1,0:T(8,128)(2,1)}, bf16[1,128,7168]{2,1,0:T(8,128)(2,1)}, u32[]{:S(2)}, u32[]{:S(2)}) collective-permute-start(bf16[1,128,7168]{2,1,0:T(8,128)(2,1)} %wo_ref), channel_id=1, source_target_pairs={{0,1},{1,0},{2,3},{3,2},{4,5},{5,4},{6,7},{7,6},{8,9},{9,8},{10,11... | collective-permute-start | bytes 5505032 | tf_op jit(solution)/shard_map/ppermute | solution.py:396
  2.5 12.6 %all-to-all-start = ((bf16[16,16,256]{2,1,0:T(8,128)(2,1)}), bf16[16,16,256]{2,1,0:T(8,128)(2,1)S(1)}, u32[]{:S(2)}, u32[]{:S(2)}) async-start(bf16[16,16,256]{2,1,0:T(8,128)(2,1)} %get-tuple-element.20), calls=%async_computation | async-start | bytes 262144 | tf_op jit(solution)/shard_map/all_to_all | solution.py:391
  10.4 6.1 %collective-permute-start.1 = (bf16[1,512,128]{2,1,0:T(8,128)(2,1)}, bf16[1,512,128]{2,1,0:T(8,128)(2,1)S(1)}, u32[]{:S(2)}, u32[]{:S(2)}) collective-permute-start(bf16[1,512,128]{2,1,0:T(8,128)(2,1)} %uv_ref), channel_id=1, source_target_pairs={{0,1},{1,0},{2,3},{3,2},{4,5},{5,4},{6,7},{7,6},{8,9},{9,8},{10,11... | collective-permute-start | bytes 393224 | tf_op jit(solution)/shard_map/ppermute | solution.py:396
  10.8 1.7 %copy-start = (bf16[2,1024,576]{1,2,0:T(8,128)(2,1)S(1)}, bf16[2,1024,576]{1,2,0:T(8,128)(2,1)}, u32[]{:S(2)}) copy-start(bf16[2,1024,576]{1,2,0:T(8,128)(2,1)} %param.13) | copy-start | bytes 7077892
  12.5 1.1 %copy-start.2 = (bf16[1,512,576]{1,2,0:T(8,128)(2,1)S(1)}, bf16[1,512,576]{1,2,0:T(8,128)(2,1)}, u32[]{:S(2)}) copy-start(bf16[1,512,576]{1,2,0:T(8,128)(2,1)} %param.10) | copy-start | bytes 1769476
  13.5 0.7 %copy-start.4 = (f32[8,640]{1,0:T(8,128)S(1)}, f32[8,640]{1,0:T(8,128)}, u32[]{:S(2)}) copy-start(f32[8,640]{1,0:T(8,128)} %get-tuple-element.21.aux_ref) | copy-start | bytes 61444
  15.1 9.7 %copy-start.5 = (s32[16]{0:T(128)S(1)}, s32[16]{0:T(128)}, u32[]{:S(2)}) copy-start(s32[16]{0:T(128)} %owners_ref.1) | copy-start | bytes 196
  24.8 12.1 %copy-start.1 = (bf16[1,128,7168]{2,1,0:T(8,128)(2,1)S(1)}, bf16[1,128,7168]{2,1,0:T(8,128)(2,1)}, u32[]{:S(2)}) copy-start(bf16[1,128,7168]{2,1,0:T(8,128)(2,1)} %wo_ref) | copy-start | bytes 5505028
  24.8 12.1 %copy-start.3 = (bf16[1,512,128]{2,1,0:T(8,128)(2,1)S(1)}, bf16[1,512,128]{2,1,0:T(8,128)(2,1)}, u32[]{:S(2)}) copy-start(bf16[1,512,128]{2,1,0:T(8,128)(2,1)} %uv_ref) | copy-start | bytes 393220
where the time goes:
time: 51.5 us; the launch traced here: 51 us
  blocking collectives  30.3 us (59%)
  Pallas kernels  8.72 us (17%)
  starting transfers between devices  8.47 us (16%)
  local copies, waits for them, and re-layouts  3.47 us (7%)
    all_to_all x3, blocking collectives, swap(): lax.all_to_all(x, 'seq', split_axis=0, concat_axis=0, axis_index_groups=[...  30.3 us
    all_to_all x1, starting transfers between devices, swap(): lax.all_to_all(x, 'seq', split_axis=0, concat_axis=0, axis_index_groups=[...  7.99 us
    unnamed x12, local copies, waits for them, and re-layouts  3.47 us
    pallas_call x1, Pallas kernels, on_device(): call(functools.partial(query_kernel, res_rows), [jax.ShapeDtypeStruct((co...  2.33 us
    pallas_call x1, Pallas kernels, on_device(): call(attend_kernel, [jax.ShapeDtypeStruct((heads, PART * (latent // LANES...  1.82 us
    pallas_call x1, Pallas kernels, on_device(): call(project_kernel, jax.ShapeDtypeStruct((seqs, 2, half + LANES), I16),...  1.61 us
    pallas_call x1, Pallas kernels, on_device(): call(functools.partial(score_kernel, scale), [jax.ShapeDtypeStruct((2 * h...  1.45 us
  transfers between devices with their start and end apart: 3, of which 0 were waited for; matrix products, arithmetic and copies ran while one was open for 0% of the time, Pallas kernels for 4%

commit v1 on v0

--- a/solution.py
+++ b/solution.py
@@ -170,12 +170,6 @@
     aux_ref[3:4, :latent] = gain_ref[...].astype(F32).reshape(1, latent)
 
 
-def fetch_start(source, target, sem, first):
-    copy = pltpu.make_async_copy(source.at[:, pl.ds(first, target.shape[1]), :], target, sem)
-    copy.start()
-    return copy
-
-
 def compress_kernel(
     res_rows, latent, aux_ref, prompt_ref, resident_hbm, out_ref, bias_ref, resident_ref, sem
 ):
@@ -217,9 +211,8 @@
 
 
 def score_kernel(
-    scale, q_ref, keys_ref, seen_ref, resident_ref, wo_hbm, sp_ref, sr_ref, stat_ref, wo_ref, sem
+    scale, q_ref, keys_ref, seen_ref, resident_ref, sp_ref, sr_ref, stat_ref
 ):
-    fetch = fetch_start(wo_hbm, wo_ref, sem, 0)
     heads = q_ref.shape[0]
     half = q_ref.shape[2]
     width = keys_ref.shape[0]
@@ -261,13 +254,11 @@
     total = jnp.sum(jnp.where(here, jnp.concatenate(sums, axis=0), 0.0), axis=0, keepdims=True)
     both = jnp.concatenate([top, total], axis=0)
     stat_ref[...] = jnp.broadcast_to(both[None], stat_ref.shape)
-    fetch.wait()
 
 
 def attend_kernel(
-    owners_ref, stat_ref, sp_ref, sr_ref, keys_ref, resident_ref, wo_hbm, out_ref, wo_ref, sem
+    owners_ref, stat_ref, sp_ref, sr_ref, keys_ref, resident_ref, _, out_ref, __
 ):
-    fetch = fetch_start(wo_hbm, wo_ref, sem, wo_ref.shape[1])
     heads = out_ref.shape[0]
     latent = out_ref.shape[1] // PART * LANES
     seqs = owners_ref.shape[0]
@@ -317,11 +308,10 @@
             for c in range(latent // LANES):
                 at = c * PART + 2 * k
                 out_ref[h, at : at + 2, :] = part[2 * h : 2 * h + 2, c * LANES : (c + 1) * LANES]
-    fetch.wait()
 
 
 def project_kernel(
-    owners_ref, part_ref, uv_ref, other_uv_ref, wo_ref, other_wo0_ref, other_wo1_ref, out_ref
+    owners_ref, part_ref, uv_ref, other_uv_ref, wo_ref, other_wo_ref, out_ref
 ):
     count, each, lanes = part_ref.shape
     seqs = owners_ref.shape[1]
@@ -354,16 +344,12 @@
     half = rest_of(iota((rows, 1), 0), 2)
     cols = wo_ref.shape[2] // 2
     product = None
-    depth = other_wo0_ref.shape[1]
-    for n, uv in enumerate((uv_ref, other_uv_ref)):
+    for n, (uv, wo) in enumerate(((uv_ref, wo_ref), (other_uv_ref, other_wo_ref))):
         head_out = dot(latent[n * rows : (n + 1) * rows], uv[0])
-        weights = [wo_ref] if n == 0 else [other_wo0_ref, other_wo1_ref]
         for side in range(2):
             lines = jnp.where(half == side, head_out, 0.0).astype(BF16)
-            for i, wo in enumerate(weights):
-                line = lines if n == 0 else lines[:, i * depth : (i + 1) * depth]
-                one = dot(line, wo[0, :, side * cols : (side + 1) * cols])
-                product = one if product is None else product + one
+            one = dot(lines, wo[0, :, side * cols : (side + 1) * cols])
+            product = one if product is None else product + one
     top = jnp.max(jnp.abs(product), axis=1, keepdims=True)
     power = jnp.clip(jnp.floor(jnp.log2(jnp.maximum(top, 1e-35))) + 1.0, -100.0, 100.0)
     coded = jnp.round(product * jnp.exp2(BITS - power)).astype(I32).astype(I16)
@@ -396,7 +382,7 @@
     return lax.ppermute(x, "seq", [(d, d ^ step) for d in range(count)])
 
 
-def call(kernel, shapes, specs, scratch=(), cost=None, room=None):
+def call(kernel, shapes, specs, scratch=(), cost=None, room=None, outs=None, aliases={}):
     single = not isinstance(shapes, (list, tuple))
     if room is None:
         room = 16 if lax.axis_size("seq") <= 32 else 56
@@ -404,7 +390,8 @@
         kernel,
         out_shape=shapes,
         in_specs=specs,
-        out_specs=VMEM if single else [VMEM] * len(shapes),
+        out_specs=VMEM if single else outs or [VMEM] * len(shapes),
+        input_output_aliases=aliases,
         scratch_shapes=list(scratch),
         cost_estimate=cost,
         compiler_params=pltpu.CompilerParams(vmem_limit_bytes=room * 1024 * 1024),
@@ -449,8 +436,6 @@
         room=60,
     )(owners_row, lengths_row, queries, w_uk[0], new_raw, kv_gain)
     received = swap(query)
-    query, w_uv, w_o = lax.optimization_barrier((query, w_uv, w_o))
-    other_uv, other_wo = trade(w_uv, 1), trade(w_o, 1)
     keys, seen, resident = call(
         functools.partial(compress_kernel, res_rows, latent),
         [
@@ -464,33 +449,33 @@
     )(aux, prompt_raw, resident)
     lanes = -(-6 * heads // LANES) * LANES
     half = out_width // 2
-    half_wo = jax.ShapeDtypeStruct((1, w_o.shape[1] // 2, out_width), BF16)
-    scores_p, scores_r, stat, other_wo0 = call(
+    scores_p, scores_r, stat = call(
         functools.partial(score_kernel, scale),
         [
             jax.ShapeDtypeStruct((2 * heads, keys_rows), F32),
             jax.ShapeDtypeStruct((2, 2 * heads, res_rows), F32),
             jax.ShapeDtypeStruct((count, 2, lanes), F32),
-            half_wo,
         ],
-        [VMEM] * 4 + [HBM],
-        [pltpu.SemaphoreType.DMA],
-    )(received, keys, seen, resident, other_wo)
-    stat, other_uv = lax.optimization_barrier((stat, other_uv))
+        [VMEM] * 4,
+    )(received, keys, seen, resident)
+    stat, w_uv, w_o = lax.optimization_barrier((stat, w_uv, w_o))
+    other_uv, other_wo = trade(w_uv, 1), trade(w_o, 1)
     stats = swap(stat)
-    part, other_wo1 = call(
+    part, other_wo = call(
         attend_kernel,
         [
             jax.ShapeDtypeStruct((heads, PART * (latent // LANES), LANES), F32),
-            half_wo,
+            jax.ShapeDtypeStruct(w_o.shape, BF16),
         ],
         [SMEM] + [VMEM] * 5 + [HBM],
-        [pltpu.SemaphoreType.DMA],
+        outs=[VMEM, HBM],
+        aliases={6: 1},
     )(owners, stats, scores_p, scores_r, keys, resident, other_wo)
+    part, other_uv = lax.optimization_barrier((part, other_uv))
     parts = swap(part)
     sums = call(
-        project_kernel, jax.ShapeDtypeStruct((seqs, 2, half + LANES), I16), [VMEM] * 7
-    )(owners_row, parts, w_uv, other_uv, w_o, other_wo0, other_wo1)
+        project_kernel, jax.ShapeDtypeStruct((seqs, 2, half + LANES), I16), [VMEM] * 6
+    )(owners_row, parts, w_uv, other_uv, w_o, other_wo)
     return call(final_kernel, jax.ShapeDtypeStruct((1, 2, out_width), BF16), [VMEM])(swap(sums))
 
 

time: 51.5 us -> 51.7 us (level)
  transfers between devices with their start and end apart: 3 -> 3, of which waited for: 0 -> 0; matrix products, arithmetic and copies ran while one was open for 0% -> 0% of each run, Pallas kernels for 4% -> 5%
where the time goes in v1:
time: 51.7 us; the launch traced here: 51.2 us
  blocking collectives  30.5 us (59%)
  starting transfers between devices  8.54 us (17%)
  Pallas kernels  8.29 us (16%)
  local copies, waits for them, and re-layouts  3.74 us (7%)
    all_to_all x3, blocking collectives, swap(): lax.all_to_all(x, 'seq', split_axis=0, concat_axis=0, axis_index_groups=[...  30.5 us
    all_to_all x1, starting transfers between devices, swap(): lax.all_to_all(x, 'seq', split_axis=0, concat_axis=0, axis_index_groups=[...  8.03 us
    unnamed x12, local copies, waits for them, and re-layouts  3.74 us
    pallas_call x1, Pallas kernels, on_device(): call(functools.partial(query_kernel, res_rows), [jax.ShapeDtypeStruct((co...  2.32 us
    pallas_call x1, Pallas kernels, on_device(): call(attend_kernel, [jax.ShapeDtypeStruct((heads, PART * (latent // LANES...  1.62 us
    pallas_call x1, Pallas kernels, on_device(): call(project_kernel, jax.ShapeDtypeStruct((seqs, 2, half + LANES), I16),...  1.58 us
    pallas_call x1, Pallas kernels, on_device(): call(functools.partial(score_kernel, scale), [jax.ShapeDtypeStruct((2 * h...  1.26 us
  transfers between devices with their start and end apart: 3, of which 0 were waited for; matrix products, arithmetic and copies ran while one was open for 0% of the time, Pallas kernels for 5%

profile of v1, /device:TPU:1, one launch (start us, length us, event | category | flops | bytes accessed | tf_op | source)
XLA Modules:
  0.0 51.2 jit_solution(1305179586214114535)
XLA Ops:
  0.0 2.3 %shard_map.100 = (bf16[16,16,256]{2,1,0:T(8,128)(2,1)}, f32[8,640]{1,0:T(8,128)}) custom-call(s32[1,16]{1,0:T(1,128)} %bitcast.8, s32[1,16]{1,0:T(1,128)} %bitcast.12, bf16[16,1,2,192]{3,2,1,0:T(2,128)(2,1)} %bitcast.11, bf16[128,512]{1,0:T(8,128)(2,1)} %bitcast.10, bf16[16,2,576]{2,1,0:T(2,128)(2,1)} %new_hbm.1, bf16[512]{0:T(512)(128)(2,1)} %gain_hbm.1), custom_call_target="tpu_custom_call" | custom-call | tf_op jit(solution)/shard_map/pallas_call | solution.py:419
  2.3 8.0 %all-to-all-start = ((bf16[16,16,256]{2,1,0:T(8,128)(2,1)}), bf16[16,16,256]{2,1,0:T(8,128)(2,1)S(1)}, u32[]{:S(2)}, u32[]{:S(2)}) async-start(bf16[16,16,256]{2,1,0:T(8,128)(2,1)} %get-tuple-element.20), calls=%async_computation | async-start | bytes 262144 | tf_op jit(solution)/shard_map/all_to_all | solution.py:377
  10.4 0.0 copy-start
  10.4 1.7 %copy-done = bf16[2,1024,576]{1,2,0:T(8,128)(2,1)S(1)} copy-done((bf16[2,1024,576]{1,2,0:T(8,128)(2,1)S(1)}, bf16[2,1024,576]{1,2,0:T(8,128)(2,1)}, u32[]{:S(2)}) %copy-start) | copy-done | bytes 2359320
  12.0 0.0 copy-start.2
  12.0 1.1 %copy-done.2 = bf16[1,512,576]{1,2,0:T(8,128)(2,1)S(1)} copy-done((bf16[1,512,576]{1,2,0:T(8,128)(2,1)S(1)}, bf16[1,512,576]{1,2,0:T(8,128)(2,1)}, u32[]{:S(2)}) %copy-start.2) | copy-done | bytes 589848
  13.1 0.0 copy-start.4
  13.1 0.7 %copy-done.4 = f32[8,640]{1,0:T(8,128)S(1)} copy-done((f32[8,640]{1,0:T(8,128)S(1)}, f32[8,640]{1,0:T(8,128)}, u32[]{:S(2)}) %copy-start.4) | copy-done | bytes 20504
  13.8 0.8 %shard_map.101 = (bf16[576,640]{1,0:T(8,128)(2,1)S(1)}, f32[8,640]{1,0:T(8,128)S(1)}, bf16[2,576,1024]{2,1,0:T(8,128)(2,1)S(1)}) custom-call(f32[8,640]{1,0:T(8,128)S(1)} %copy-done.4, bf16[1,576,512]{2,1,0:T(8,128)(2,1)S(1)} %bitcast.7, bf16[2,576,1024]{2,1,0:T(8,128)(2,1)S(1)} %bitcast.6), custom_call_target="tpu_custom_call" | custom-call | flops 10000000 | bytes 10000000 | tf_op jit(solution)/shard_map/pallas_call | solution.py:439
  14.6 0.0 copy-start.3
  14.6 0.0 copy-start.5
  14.6 0.0 all-to-all-done.q_ref
  14.6 0.0 copy-start.1
  14.6 1.3 %shard_map.102 = (f32[32,640]{1,0:T(8,128)S(1)}, f32[2,32,1024]{2,1,0:T(8,128)S(1)}, f32[16,2,128]{2,1,0:T(2,128)S(1)}) custom-call(bf16[16,16,256]{2,1,0:T(8,128)(2,1)S(1)} %all-to-all-done.q_ref, bf16[576,640]{1,0:T(8,128)(2,1)S(1)} %get-tuple-element.22.keys_ref, f32[8,640]{1,0:T(8,128)S(1)} %get-tuple-element.23.seen_ref, ...), custom_call_target="tpu_custom_call" | custom-call | tf_op jit(solution)/shard_map/pallas_call | solution.py:452
  15.9 0.3 copy-done.1
  16.2 0.4 collective-permute-start
  16.5 0.0 copy-done.3
  16.5 0.1 collective-permute-start.1
  16.7 8.5 %all_to_all.20.stat_ref = f32[16,2,128]{2,1,0:T(2,128)S(1)} all-to-all(f32[16,2,128]{2,1,0:T(2,128)S(1)} %get-tuple-element.26), channel_id=1, replica_groups={{10,11,8,9,14,15,12,13,2,3,0,1,6,7,4,5},{26,27,24,25,30,31,28,29,18,19,..., dimensions={0} | all-to-all | bytes 32768 | tf_op jit(solution)/shard_map/all_to_all | solution.py:377
  25.2 0.0 collective-permute-done._
  25.2 0.0 copy-done.5
  25.2 1.6 %shard_map.103 = (f32[16,24,128]{2,1,0:T(8,128)S(1)}, bf16[1,128,7168]{2,1,0:T(8,128)(2,1)S(1)}) custom-call(s32[16]{0:T(128)S(1)} %copy-done.5, f32[16,2,128]{2,1,0:T(2,128)S(1)} %all_to_all.20.stat_ref, f32[32,640]{1,0:T(8,128)S(1)} %get-tuple-element.27.sp_ref, f32[2,32,1024]{2,1,0:T(8,128)S(1)} %get-tuple-element.28.sr_ref, ...), custom_call_target="tpu_custom_call", output_to_operand_aliasing={{1}: (6, {})} | custom-call | tf_op jit(solution)/shard_map/pallas_call | solution.py:464
  26.8 0.0 collective-permute-done.1.other_uv_ref
  26.8 10.3 %all_to_all.21.part_ref = f32[16,24,128]{2,1,0:T(8,128)S(1)} all-to-all(f32[16,24,128]{2,1,0:T(8,128)S(1)} %get-tuple-element.32), channel_id=1, replica_groups={{10,11,8,9,14,15,12,13,2,3,0,1,6,7,4,5},{26,27,24,25,30,31,28,29,18,19,..., dimensions={0} | all-to-all | bytes 393216 | tf_op jit(solution)/shard_map/all_to_all | solution.py:377
  37.1 1.6 %shard_map.104 = s16[16,2,3712]{2,1,0:T(2,128)(2,1)S(1)} custom-call(s32[1,16]{1,0:T(1,128)S(1)} %bitcast.9, f32[16,24,128]{2,1,0:T(8,128)S(1)} %all_to_all.21.part_ref, bf16[1,512,128]{2,1,0:T(8,128)(2,1)S(1)} %copy-done.3, bf16[1,512,128]{2,1,0:T(8,128)(2,1)S(1)} %collective-permute-done.1.other_uv_ref, bf16[1,128,7168]{2,1,0:T(8,128)(2,1)S(1)} %copy-done.1, ...), custom_call_target="tpu_custom_call" | custom-call | tf_op jit(solution)/shard_map/pallas_call | solution.py:476
  38.7 11.7 %all_to_all.22.in_ref = s16[16,2,3712]{2,1,0:T(2,128)(2,1)S(1)} all-to-all(s16[16,2,3712]{2,1,0:T(2,128)(2,1)S(1)} %shard_map.104), channel_id=1, replica_groups={{10,11,8,9,14,15,12,13,2,3,0,1,6,7,4,5},{26,27,24,25,30,31,28,29,18,19,..., dimensions={0} | all-to-all | bytes 475136 | tf_op jit(solution)/shard_map/all_to_all | solution.py:377
  50.5 0.8 %shard_map.105 = bf16[1,2,7168]{2,1,0:T(2,128)(2,1)} custom-call(s16[16,2,3712]{2,1,0:T(2,128)(2,1)S(1)} %all_to_all.22.in_ref), custom_call_target="tpu_custom_call" | custom-call | tf_op jit(solution)/shard_map/pallas_call | solution.py:479
Async XLA Ops:
  2.3 12.3 %all-to-all-start = ((bf16[16,16,256]{2,1,0:T(8,128)(2,1)}), bf16[16,16,256]{2,1,0:T(8,128)(2,1)S(1)}, u32[]{:S(2)}, u32[]{:S(2)}) async-start(bf16[16,16,256]{2,1,0:T(8,128)(2,1)} %get-tuple-element.20), calls=%async_computation | async-start | bytes 262144 | tf_op jit(solution)/shard_map/all_to_all | solution.py:377
  10.4 1.7 %copy-start = (bf16[2,1024,576]{1,2,0:T(8,128)(2,1)S(1)}, bf16[2,1024,576]{1,2,0:T(8,128)(2,1)}, u32[]{:S(2)}) copy-start(bf16[2,1024,576]{1,2,0:T(8,128)(2,1)} %param.13) | copy-start | bytes 7077892
  12.0 1.1 %copy-start.2 = (bf16[1,512,576]{1,2,0:T(8,128)(2,1)S(1)}, bf16[1,512,576]{1,2,0:T(8,128)(2,1)}, u32[]{:S(2)}) copy-start(bf16[1,512,576]{1,2,0:T(8,128)(2,1)} %param.10) | copy-start | bytes 1769476
  13.1 0.7 %copy-start.4 = (f32[8,640]{1,0:T(8,128)S(1)}, f32[8,640]{1,0:T(8,128)}, u32[]{:S(2)}) copy-start(f32[8,640]{1,0:T(8,128)} %get-tuple-element.21.aux_ref) | copy-start | bytes 61444
  14.6 1.9 %copy-start.3 = (bf16[1,512,128]{2,1,0:T(8,128)(2,1)S(1)}, bf16[1,512,128]{2,1,0:T(8,128)(2,1)}, u32[]{:S(2)}) copy-start(bf16[1,512,128]{2,1,0:T(8,128)(2,1)} %uv_ref) | copy-start | bytes 393220
  14.6 10.6 %copy-start.5 = (s32[16]{0:T(128)S(1)}, s32[16]{0:T(128)}, u32[]{:S(2)}) copy-start(s32[16]{0:T(128)} %owners_ref.1) | copy-start | bytes 196
  14.6 1.5 %copy-start.1 = (bf16[1,128,7168]{2,1,0:T(8,128)(2,1)S(1)}, bf16[1,128,7168]{2,1,0:T(8,128)(2,1)}, u32[]{:S(2)}) copy-start(bf16[1,128,7168]{2,1,0:T(8,128)(2,1)} %wo_ref) | copy-start | bytes 5505028
  16.2 9.0 %collective-permute-start = (bf16[1,128,7168]{2,1,0:T(8,128)(2,1)S(1)}, bf16[1,128,7168]{2,1,0:T(8,128)(2,1)S(1)}, u32[]{:S(2)}, u32[]{:S(2)}) collective-permute-start(bf16[1,128,7168]{2,1,0:T(8,128)(2,1)S(1)} %copy-done.1), channel_id=1, source_target_pairs={{0,1},{1,0},{2,3},{3,2},{4,5},{5,4},{6,7},{7,6},{8,9},{9,8},{10,11... | collective-permute-start | bytes 5505032 | tf_op jit(solution)/shard_map/ppermute | solution.py:382
  16.5 10.3 %collective-permute-start.1 = (bf16[1,512,128]{2,1,0:T(8,128)(2,1)S(1)}, bf16[1,512,128]{2,1,0:T(8,128)(2,1)S(1)}, u32[]{:S(2)}, u32[]{:S(2)}) collective-permute-start(bf16[1,512,128]{2,1,0:T(8,128)(2,1)S(1)} %copy-done.3), channel_id=1, source_target_pairs={{0,1},{1,0},{2,3},{3,2},{4,5},{5,4},{6,7},{7,6},{8,9},{9,8},{10,11... | collective-permute-start | bytes 393224 | tf_op jit(solution)/shard_map/ppermute | solution.py:382

commit v2 on v1

--- a/solution.py
+++ b/solution.py
@@ -146,21 +146,26 @@
     owners = owners_ref[...]
     owner = doubled(owners, 5)
     slot = doubled(slots_of(owners), 5)
-    shape = (out_ref.shape[0] * PACK, 5 * rows)
-    dest, r = over(iota(shape, 0), PACK) ^ shift_of(out_ref.shape[0]), rest_of(iota(shape, 0), PACK)
-    lane = iota((1, 5 * rows), 1)
+    count = out_ref.shape[0]
+    shape = (count, 5 * rows)
+    dest = iota(shape, 0) ^ shift_of(count)
+    lane = iota(shape, 1)
     piece, seq, tok = over(lane, rows), over(rest_of(lane, rows), 2), rest_of(lane, 2)
-    start = jnp.where(piece < 2, piece * PART, 2 * PART) + tok
-    offset = r - start
-    rotary = piece >= 2
     third = piece - 2
-    here = jnp.where(owner == dest, slot + 1, jnp.where(seq == dest, 0, -1))
-    both = (owner == dest) & (seq == dest)
-    wide = (offset == 2 * here) | (both & (offset == 0))
-    narrow = (offset == 0) & ((here == third) | (both & (third == 0)))
-    hit = (~rotary & (here >= 0) & wide) | (rotary & narrow)
+    first = jnp.where(piece < 2, piece * PART, 2 * PART) + tok
+    own = seq == dest
+    here = jnp.where(owner == dest, slot + 1, jnp.where(own, 0, -1))
+    wide = jnp.where(here >= 0, first + 2 * here, -1)
+    target = jnp.where(piece < 2, wide, jnp.where(here == third, first, -1))
+    again = jnp.where((owner == dest) & own & ((piece < 2) | (third == 0)), first, -1)
+    r = iota((PACK, 5 * rows), 0)
+    hits = []
+    for d in range(count):
+        hit = (r == target[d : d + 1]) | (r == again[d : d + 1])
+        hits.append(jnp.where(hit, 1.0, 0.0).astype(BF16))
+    hit = jnp.concatenate(hits, axis=0)
     pieces = jnp.concatenate(pieces, axis=0)
-    result = dot(jnp.where(hit, 1.0, 0.0).astype(BF16), pieces)
+    result = dot(hit, pieces)
     out_ref[...] = result.astype(BF16).reshape(out_ref.shape)
     width = new_ref.shape[1]
     aux_ref[0:2, :width] = new_ref[...].astype(F32)
@@ -436,6 +441,8 @@
         room=60,
     )(owners_row, lengths_row, queries, w_uk[0], new_raw, kv_gain)
     received = swap(query)
+    query, w_uv = lax.optimization_barrier((query, w_uv))
+    other_uv = trade(w_uv, 1)
     keys, seen, resident = call(
         functools.partial(compress_kernel, res_rows, latent),
         [
@@ -458,8 +465,8 @@
         ],
         [VMEM] * 4,
     )(received, keys, seen, resident)
-    stat, w_uv, w_o = lax.optimization_barrier((stat, w_uv, w_o))
-    other_uv, other_wo = trade(w_uv, 1), trade(w_o, 1)
+    stat, other_uv, w_o = lax.optimization_barrier((stat, other_uv, w_o))
+    other_wo = trade(w_o, 1)
     stats = swap(stat)
     part, other_wo = call(
         attend_kernel,
@@ -471,7 +478,6 @@
         outs=[VMEM, HBM],
         aliases={6: 1},
     )(owners, stats, scores_p, scores_r, keys, resident, other_wo)
-    part, other_uv = lax.optimization_barrier((part, other_uv))
     parts = swap(part)
     sums = call(
         project_kernel, jax.ShapeDtypeStruct((seqs, 2, half + LANES), I16), [VMEM] * 6

time: 51.7 us -> 51 us (0.986)
  transfers between devices with their start and end apart: 3 -> 3, of which waited for: 0 -> 0; matrix products, arithmetic and copies ran while one was open for 0% -> 0% of each run, Pallas kernels for 5% -> 4%
where the time goes in v2:
time: 51 us; the launch traced here: 50.5 us
  blocking collectives  30.2 us (59%)
  starting transfers between devices  8.54 us (17%)
  Pallas kernels  8.02 us (16%)
  local copies, waits for them, and re-layouts  3.69 us (7%)
    all_to_all x3, blocking collectives, swap(): lax.all_to_all(x, 'seq', split_axis=0, concat_axis=0, axis_index_groups=[...  30.2 us
    all_to_all x1, starting transfers between devices, swap(): lax.all_to_all(x, 'seq', split_axis=0, concat_axis=0, axis_index_groups=[...  8.03 us
    unnamed x12, local copies, waits for them, and re-layouts  3.69 us
    pallas_call x1, Pallas kernels, on_device(): call(functools.partial(query_kernel, res_rows), [jax.ShapeDtypeStruct((co...  2.04 us
    pallas_call x1, Pallas kernels, on_device(): call(attend_kernel, [jax.ShapeDtypeStruct((heads, PART * (latent // LANES...  1.63 us
    pallas_call x1, Pallas kernels, on_device(): call(project_kernel, jax.ShapeDtypeStruct((seqs, 2, half + LANES), I16),...  1.58 us
    pallas_call x1, Pallas kernels, on_device(): call(functools.partial(score_kernel, scale), [jax.ShapeDtypeStruct((2 * h...  1.26 us
  transfers between devices with their start and end apart: 3, of which 0 were waited for; matrix products, arithmetic and copies ran while one was open for 0% of the time, Pallas kernels for 4%

profile of v2, /device:TPU:1, one launch (start us, length us, event | category | flops | bytes accessed | tf_op | source)
XLA Modules:
  0.0 50.5 jit_solution(11199854437559856710)
XLA Ops:
  0.0 2.0 %shard_map.100 = (bf16[16,16,256]{2,1,0:T(8,128)(2,1)}, f32[8,640]{1,0:T(8,128)}) custom-call(s32[1,16]{1,0:T(1,128)} %bitcast.8, s32[1,16]{1,0:T(1,128)} %bitcast.12, bf16[16,1,2,192]{3,2,1,0:T(2,128)(2,1)} %bitcast.11, bf16[128,512]{1,0:T(8,128)(2,1)} %bitcast.10, bf16[16,2,576]{2,1,0:T(2,128)(2,1)} %new_hbm.1, bf16[512]{0:T(512)(128)(2,1)} %gain_hbm.1), custom_call_target="tpu_custom_call" | custom-call | tf_op jit(solution)/shard_map/pallas_call | solution.py:424
  2.0 8.0 %all-to-all-start = ((bf16[16,16,256]{2,1,0:T(8,128)(2,1)}), bf16[16,16,256]{2,1,0:T(8,128)(2,1)S(1)}, u32[]{:S(2)}, u32[]{:S(2)}) async-start(bf16[16,16,256]{2,1,0:T(8,128)(2,1)} %get-tuple-element.19), calls=%async_computation | async-start | bytes 262144 | tf_op jit(solution)/shard_map/all_to_all | solution.py:382
  10.1 0.4 collective-permute-start
  10.4 0.0 copy-start
  10.4 1.7 %copy-done = bf16[2,1024,576]{1,2,0:T(8,128)(2,1)S(1)} copy-done((bf16[2,1024,576]{1,2,0:T(8,128)(2,1)S(1)}, bf16[2,1024,576]{1,2,0:T(8,128)(2,1)}, u32[]{:S(2)}) %copy-start) | copy-done | bytes 2359320
  12.1 0.0 copy-start.2
  12.1 1.1 %copy-done.2 = bf16[1,512,576]{1,2,0:T(8,128)(2,1)S(1)} copy-done((bf16[1,512,576]{1,2,0:T(8,128)(2,1)S(1)}, bf16[1,512,576]{1,2,0:T(8,128)(2,1)}, u32[]{:S(2)}) %copy-start.2) | copy-done | bytes 589848
  13.2 0.0 copy-start.4
  13.2 0.7 %copy-done.4 = f32[8,640]{1,0:T(8,128)S(1)} copy-done((f32[8,640]{1,0:T(8,128)S(1)}, f32[8,640]{1,0:T(8,128)}, u32[]{:S(2)}) %copy-start.4) | copy-done | bytes 20504
  13.9 0.8 %shard_map.101 = (bf16[576,640]{1,0:T(8,128)(2,1)S(1)}, f32[8,640]{1,0:T(8,128)S(1)}, bf16[2,576,1024]{2,1,0:T(8,128)(2,1)S(1)}) custom-call(f32[8,640]{1,0:T(8,128)S(1)} %copy-done.4, bf16[1,576,512]{2,1,0:T(8,128)(2,1)S(1)} %bitcast.7, bf16[2,576,1024]{2,1,0:T(8,128)(2,1)S(1)} %bitcast.6), custom_call_target="tpu_custom_call" | custom-call | flops 10000000 | bytes 10000000 | tf_op jit(solution)/shard_map/pallas_call | solution.py:446
  14.7 0.0 copy-start.5
  14.7 0.0 all-to-all-done.q_ref
  14.7 0.0 copy-start.1
  14.7 1.3 %shard_map.102 = (f32[32,640]{1,0:T(8,128)S(1)}, f32[2,32,1024]{2,1,0:T(8,128)S(1)}, f32[16,2,128]{2,1,0:T(2,128)S(1)}) custom-call(bf16[16,16,256]{2,1,0:T(8,128)(2,1)S(1)} %all-to-all-done.q_ref, bf16[576,640]{1,0:T(8,128)(2,1)S(1)} %get-tuple-element.21.keys_ref, f32[8,640]{1,0:T(8,128)S(1)} %get-tuple-element.22.seen_ref, ...), custom_call_target="tpu_custom_call" | custom-call | tf_op jit(solution)/shard_map/pallas_call | solution.py:459
  16.0 0.0 collective-permute-done.other_uv_ref
  16.0 0.2 copy-done.1
  16.2 0.1 collective-permute-start.1
  16.3 8.2 %all_to_all.20.stat_ref = f32[16,2,128]{2,1,0:T(2,128)S(1)} all-to-all(f32[16,2,128]{2,1,0:T(2,128)S(1)} %get-tuple-element.26), channel_id=1, replica_groups={{10,11,8,9,14,15,12,13,2,3,0,1,6,7,4,5},{26,27,24,25,30,31,28,29,18,19,..., dimensions={0} | all-to-all | bytes 32768 | tf_op jit(solution)/shard_map/all_to_all | solution.py:382
  24.5 0.0 collective-permute-done.1._
  24.5 0.0 copy-done.5
  24.5 0.0 copy-start.3
  24.5 1.6 %shard_map.103 = (f32[16,24,128]{2,1,0:T(8,128)S(1)}, bf16[1,128,7168]{2,1,0:T(8,128)(2,1)S(1)}) custom-call(s32[16]{0:T(128)S(1)} %copy-done.5, f32[16,2,128]{2,1,0:T(2,128)S(1)} %all_to_all.20.stat_ref, f32[32,640]{1,0:T(8,128)S(1)} %get-tuple-element.27.sp_ref, f32[2,32,1024]{2,1,0:T(8,128)S(1)} %get-tuple-element.28.sr_ref, ...), custom_call_target="tpu_custom_call", output_to_operand_aliasing={{1}: (6, {})} | custom-call | tf_op jit(solution)/shard_map/pallas_call | solution.py:471
  26.2 10.3 %all_to_all.21.part_ref = f32[16,24,128]{2,1,0:T(8,128)S(1)} all-to-all(f32[16,24,128]{2,1,0:T(8,128)S(1)} %get-tuple-element.30), channel_id=1, replica_groups={{10,11,8,9,14,15,12,13,2,3,0,1,6,7,4,5},{26,27,24,25,30,31,28,29,18,19,..., dimensions={0} | all-to-all | bytes 393216 | tf_op jit(solution)/shard_map/all_to_all | solution.py:382
  36.5 0.0 copy-done.3
  36.5 1.6 %shard_map.104 = s16[16,2,3712]{2,1,0:T(2,128)(2,1)S(1)} custom-call(s32[1,16]{1,0:T(1,128)S(1)} %bitcast.9, f32[16,24,128]{2,1,0:T(8,128)S(1)} %all_to_all.21.part_ref, bf16[1,512,128]{2,1,0:T(8,128)(2,1)S(1)} %copy-done.3, bf16[1,512,128]{2,1,0:T(8,128)(2,1)S(1)} %collective-permute-done.other_uv_ref, bf16[1,128,7168]{2,1,0:T(8,128)(2,1)S(1)} %copy-done.1, ...), custom_call_target="tpu_custom_call" | custom-call | tf_op jit(solution)/shard_map/pallas_call | solution.py:482
  38.1 11.7 %all_to_all.22.in_ref = s16[16,2,3712]{2,1,0:T(2,128)(2,1)S(1)} all-to-all(s16[16,2,3712]{2,1,0:T(2,128)(2,1)S(1)} %shard_map.104), channel_id=1, replica_groups={{10,11,8,9,14,15,12,13,2,3,0,1,6,7,4,5},{26,27,24,25,30,31,28,29,18,19,..., dimensions={0} | all-to-all | bytes 475136 | tf_op jit(solution)/shard_map/all_to_all | solution.py:382
  49.8 0.8 %shard_map.105 = bf16[1,2,7168]{2,1,0:T(2,128)(2,1)} custom-call(s16[16,2,3712]{2,1,0:T(2,128)(2,1)S(1)} %all_to_all.22.in_ref), custom_call_target="tpu_custom_call" | custom-call | tf_op jit(solution)/shard_map/pallas_call | solution.py:485
Async XLA Ops:
  2.0 12.6 %all-to-all-start = ((bf16[16,16,256]{2,1,0:T(8,128)(2,1)}), bf16[16,16,256]{2,1,0:T(8,128)(2,1)S(1)}, u32[]{:S(2)}, u32[]{:S(2)}) async-start(bf16[16,16,256]{2,1,0:T(8,128)(2,1)} %get-tuple-element.19), calls=%async_computation | async-start | bytes 262144 | tf_op jit(solution)/shard_map/all_to_all | solution.py:382
  10.1 5.9 %collective-permute-start = (bf16[1,512,128]{2,1,0:T(8,128)(2,1)}, bf16[1,512,128]{2,1,0:T(8,128)(2,1)S(1)}, u32[]{:S(2)}, u32[]{:S(2)}) collective-permute-start(bf16[1,512,128]{2,1,0:T(8,128)(2,1)} %uv_ref), channel_id=1, source_target_pairs={{0,1},{1,0},{2,3},{3,2},{4,5},{5,4},{6,7},{7,6},{8,9},{9,8},{10,11... | collective-permute-start | bytes 393224 | tf_op jit(solution)/shard_map/ppermute | solution.py:387
  10.4 1.7 %copy-start = (bf16[2,1024,576]{1,2,0:T(8,128)(2,1)S(1)}, bf16[2,1024,576]{1,2,0:T(8,128)(2,1)}, u32[]{:S(2)}) copy-start(bf16[2,1024,576]{1,2,0:T(8,128)(2,1)} %param.13) | copy-start | bytes 7077892
  12.1 1.1 %copy-start.2 = (bf16[1,512,576]{1,2,0:T(8,128)(2,1)S(1)}, bf16[1,512,576]{1,2,0:T(8,128)(2,1)}, u32[]{:S(2)}) copy-start(bf16[1,512,576]{1,2,0:T(8,128)(2,1)} %param.10) | copy-start | bytes 1769476
  13.2 0.7 %copy-start.4 = (f32[8,640]{1,0:T(8,128)S(1)}, f32[8,640]{1,0:T(8,128)}, u32[]{:S(2)}) copy-start(f32[8,640]{1,0:T(8,128)} %get-tuple-element.20.aux_ref) | copy-start | bytes 61444
  14.7 9.9 %copy-start.5 = (s32[16]{0:T(128)S(1)}, s32[16]{0:T(128)}, u32[]{:S(2)}) copy-start(s32[16]{0:T(128)} %owners_ref.1) | copy-start | bytes 196
  14.7 1.5 %copy-start.1 = (bf16[1,128,7168]{2,1,0:T(8,128)(2,1)S(1)}, bf16[1,128,7168]{2,1,0:T(8,128)(2,1)}, u32[]{:S(2)}) copy-start(bf16[1,128,7168]{2,1,0:T(8,128)(2,1)} %wo_ref) | copy-start | bytes 5505028
  16.2 8.3 %collective-permute-start.1 = (bf16[1,128,7168]{2,1,0:T(8,128)(2,1)S(1)}, bf16[1,128,7168]{2,1,0:T(8,128)(2,1)S(1)}, u32[]{:S(2)}, u32[]{:S(2)}) collective-permute-start(bf16[1,128,7168]{2,1,0:T(8,128)(2,1)S(1)} %copy-done.1), channel_id=1, source_target_pairs={{0,1},{1,0},{2,3},{3,2},{4,5},{5,4},{6,7},{7,6},{8,9},{9,8},{10,11... | collective-permute-start | bytes 5505032 | tf_op jit(solution)/shard_map/ppermute | solution.py:387
  24.5 11.9 %copy-start.3 = (bf16[1,512,128]{2,1,0:T(8,128)(2,1)S(1)}, bf16[1,512,128]{2,1,0:T(8,128)(2,1)}, u32[]{:S(2)}) copy-start(bf16[1,512,128]{2,1,0:T(8,128)(2,1)} %uv_ref) | copy-start | bytes 393220

commit v3 on v2

--- a/solution.py
+++ b/solution.py
@@ -67,10 +67,13 @@
 def frequencies(half, shape, dim):
     at = rest_of(iota(shape, dim), half)
     values = np.float32(10000.0) ** (-(np.arange(half, dtype=np.float32) * np.float32(2.0)) / np.float32(2 * half))
-    result = jnp.zeros(shape, F32)
-    for i in range(half):
-        result = jnp.where(at == i, float(values[i]), result)
-    return result
+    level = [jnp.full(shape, float(v), F32) for v in values]
+    bit = 1
+    while len(level) > 1:
+        odd = (at & bit) != 0
+        level = [jnp.where(odd, b, a) for a, b in zip(level[::2], level[1::2])]
+        bit *= 2
+    return level[0]
 
 
 def sine_cosine(angle):
@@ -262,7 +265,7 @@
 
 
 def attend_kernel(
-    owners_ref, stat_ref, sp_ref, sr_ref, keys_ref, resident_ref, _, out_ref, __
+    owners_ref, stat_ref, sp_ref, sr_ref, keys_ref, resident_ref, out_ref
 ):
     heads = out_ref.shape[0]
     latent = out_ref.shape[1] // PART * LANES
@@ -324,17 +327,21 @@
     rows = 2 * seqs
     core = lax.axis_index("seq") % 2
     owners = owners_ref[...]
-    row = iota((cuts * 2 * rows, 1), 0)
-    cut, other, seq = over(row, 2 * rows), over(rest_of(row, 2 * rows), rows), over(rest_of(row, rows), 2)
+    row = iota((2 * rows, 1), 0)
     shift = shift_of(count)
-    seq = seq ^ shift
+    other, place = over(row, rows), over(rest_of(row, rows), 2)
+    seq = place ^ shift
     head = jnp.where(other == 0, core, 1 - core)
     owner = column_of(owners, seq)
     slot = column_of(slots_of(owners), seq)
-    first = (seq ^ shift) * each + cut * PART + head
-    second = (owner ^ shift) * each + cut * PART + 2 + 2 * slot + head
-    at = iota((cuts * 2 * rows, count * each), 1)
-    hit = jnp.where((at == first) | (at == second), 1.0, 0.0).astype(BF16)
+    shape = (2 * rows, count * each)
+    first = jnp.broadcast_to(place * each + head, shape)
+    second = jnp.broadcast_to((owner ^ shift) * each + 2 + 2 * slot + head, shape)
+    hits = []
+    for cut in range(cuts):
+        at = iota(shape, 1) - cut * PART
+        hits.append(jnp.where((at == first) | (at == second), 1.0, 0.0).astype(BF16))
+    hit = jnp.concatenate(hits, axis=0)
     rest = part_ref[...].reshape(count * each, lanes)
     latent = None
     for _ in range(3):
@@ -387,7 +394,7 @@
     return lax.ppermute(x, "seq", [(d, d ^ step) for d in range(count)])
 
 
-def call(kernel, shapes, specs, scratch=(), cost=None, room=None, outs=None, aliases={}):
+def call(kernel, shapes, specs, scratch=(), cost=None, room=None):
     single = not isinstance(shapes, (list, tuple))
     if room is None:
         room = 16 if lax.axis_size("seq") <= 32 else 56
@@ -395,8 +402,7 @@
         kernel,
         out_shape=shapes,
         in_specs=specs,
-        out_specs=VMEM if single else outs or [VMEM] * len(shapes),
-        input_output_aliases=aliases,
+        out_specs=VMEM if single else [VMEM] * len(shapes),
         scratch_shapes=list(scratch),
         cost_estimate=cost,
         compiler_params=pltpu.CompilerParams(vmem_limit_bytes=room * 1024 * 1024),
@@ -465,19 +471,15 @@
         ],
         [VMEM] * 4,
     )(received, keys, seen, resident)
-    stat, other_uv, w_o = lax.optimization_barrier((stat, other_uv, w_o))
+    stat, other_uv = lax.optimization_barrier((stat, other_uv))
+    stats = swap(stat)
+    part = call(
+        attend_kernel,
+        jax.ShapeDtypeStruct((heads, PART * (latent // LANES), LANES), F32),
+        [SMEM] + [VMEM] * 5,
+    )(owners, stats, scores_p, scores_r, keys, resident)
+    part, w_o = lax.optimization_barrier((part, w_o))
     other_wo = trade(w_o, 1)
-    stats = swap(stat)
-    part, other_wo = call(
-        attend_kernel,
-        [
-            jax.ShapeDtypeStruct((heads, PART * (latent // LANES), LANES), F32),
-            jax.ShapeDtypeStruct(w_o.shape, BF16),
-        ],
-        [SMEM] + [VMEM] * 5 + [HBM],
-        outs=[VMEM, HBM],
-        aliases={6: 1},
-    )(owners, stats, scores_p, scores_r, keys, resident, other_wo)
     parts = swap(part)
     sums = call(
         project_kernel, jax.ShapeDtypeStruct((seqs, 2, half + LANES), I16), [VMEM] * 6

time: 51 us -> 50.9 us (level)
  no operation moved by 1% of the time
where the time goes in v3:
time: 50.9 us; the launch traced here: 50.4 us
  blocking collectives  30.2 us (59%)
  starting transfers between devices  8.85 us (17%)
  Pallas kernels  7.84 us (15%)
  local copies, waits for them, and re-layouts  3.47 us (7%)
    all_to_all x3, blocking collectives, swap(): lax.all_to_all(x, 'seq', split_axis=0, concat_axis=0, axis_index_groups=[...  30.2 us
    all_to_all x1, starting transfers between devices, swap(): lax.all_to_all(x, 'seq', split_axis=0, concat_axis=0, axis_index_groups=[...  8.03 us
    unnamed x12, local copies, waits for them, and re-layouts  3.47 us
    pallas_call x1, Pallas kernels, on_device(): call(functools.partial(query_kernel, res_rows), [jax.ShapeDtypeStruct((co...  2.04 us
    pallas_call x1, Pallas kernels, on_device(): call(attend_kernel, jax.ShapeDtypeStruct((heads, PART * (latent // LANES)...  1.62 us
    pallas_call x1, Pallas kernels, on_device(): call(project_kernel, jax.ShapeDtypeStruct((seqs, 2, half + LANES), I16),...  1.5 us
    pallas_call x1, Pallas kernels, on_device(): call(functools.partial(score_kernel, scale), [jax.ShapeDtypeStruct((2 * h...  1.26 us
  transfers between devices with their start and end apart: 3, of which 0 were waited for; matrix products, arithmetic and copies ran while one was open for 0% of the time, Pallas kernels for 4%

profile of v3, /device:TPU:1, one launch (start us, length us, event | category | flops | bytes accessed | tf_op | source)
XLA Modules:
  0.0 50.4 jit_solution(5546366177896311465)
XLA Ops:
  0.0 2.0 %shard_map.100 = (bf16[16,16,256]{2,1,0:T(8,128)(2,1)}, f32[8,640]{1,0:T(8,128)}) custom-call(s32[1,16]{1,0:T(1,128)} %bitcast.8, s32[1,16]{1,0:T(1,128)} %bitcast.12, bf16[16,1,2,192]{3,2,1,0:T(2,128)(2,1)} %bitcast.11, bf16[128,512]{1,0:T(8,128)(2,1)} %bitcast.10, bf16[16,2,576]{2,1,0:T(2,128)(2,1)} %new_hbm.1, bf16[512]{0:T(512)(128)(2,1)} %gain_hbm.1), custom_call_target="tpu_custom_call" | custom-call | tf_op jit(solution)/shard_map/pallas_call | solution.py:430
  2.0 8.0 %all-to-all-start = ((bf16[16,16,256]{2,1,0:T(8,128)(2,1)}), bf16[16,16,256]{2,1,0:T(8,128)(2,1)S(1)}, u32[]{:S(2)}, u32[]{:S(2)}) async-start(bf16[16,16,256]{2,1,0:T(8,128)(2,1)} %get-tuple-element.18), calls=%async_computation | async-start | bytes 262144 | tf_op jit(solution)/shard_map/all_to_all | solution.py:389
  10.1 0.4 collective-permute-start
  10.4 0.0 copy-start
  10.4 1.7 %copy-done = bf16[2,1024,576]{1,2,0:T(8,128)(2,1)S(1)} copy-done((bf16[2,1024,576]{1,2,0:T(8,128)(2,1)S(1)}, bf16[2,1024,576]{1,2,0:T(8,128)(2,1)}, u32[]{:S(2)}) %copy-start) | copy-done | bytes 2359320
  12.1 0.0 copy-start.2
  12.1 1.1 %copy-done.2 = bf16[1,512,576]{1,2,0:T(8,128)(2,1)S(1)} copy-done((bf16[1,512,576]{1,2,0:T(8,128)(2,1)S(1)}, bf16[1,512,576]{1,2,0:T(8,128)(2,1)}, u32[]{:S(2)}) %copy-start.2) | copy-done | bytes 589848
  13.2 0.0 copy-start.4
  13.2 0.7 %copy-done.4 = f32[8,640]{1,0:T(8,128)S(1)} copy-done((f32[8,640]{1,0:T(8,128)S(1)}, f32[8,640]{1,0:T(8,128)}, u32[]{:S(2)}) %copy-start.4) | copy-done | bytes 20504
  13.9 0.7 %shard_map.101 = (bf16[576,640]{1,0:T(8,128)(2,1)S(1)}, f32[8,640]{1,0:T(8,128)S(1)}, bf16[2,576,1024]{2,1,0:T(8,128)(2,1)S(1)}) custom-call(f32[8,640]{1,0:T(8,128)S(1)} %copy-done.4, bf16[1,576,512]{2,1,0:T(8,128)(2,1)S(1)} %bitcast.7, bf16[2,576,1024]{2,1,0:T(8,128)(2,1)S(1)} %bitcast.6), custom_call_target="tpu_custom_call" | custom-call | flops 10000000 | bytes 10000000 | tf_op jit(solution)/shard_map/pallas_call | solution.py:452
  14.6 0.0 copy-start.5
  14.6 0.0 all-to-all-done.q_ref
  14.6 1.3 %shard_map.102 = (f32[32,640]{1,0:T(8,128)S(1)}, f32[2,32,1024]{2,1,0:T(8,128)S(1)}, f32[16,2,128]{2,1,0:T(2,128)S(1)}) custom-call(bf16[16,16,256]{2,1,0:T(8,128)(2,1)S(1)} %all-to-all-done.q_ref, bf16[576,640]{1,0:T(8,128)(2,1)S(1)} %get-tuple-element.20.keys_ref, f32[8,640]{1,0:T(8,128)S(1)} %get-tuple-element.21.seen_ref, ...), custom_call_target="tpu_custom_call" | custom-call | tf_op jit(solution)/shard_map/pallas_call | solution.py:465
  15.9 0.0 copy-start.1
  15.9 0.0 copy-start.3
  15.9 0.0 collective-permute-done.other_uv_ref
  15.9 8.4 %all_to_all.20.stat_ref = f32[16,2,128]{2,1,0:T(2,128)S(1)} all-to-all(f32[16,2,128]{2,1,0:T(2,128)S(1)} %get-tuple-element.25), channel_id=1, replica_groups={{10,11,8,9,14,15,12,13,2,3,0,1,6,7,4,5},{26,27,24,25,30,31,28,29,18,19,..., dimensions={0} | all-to-all | bytes 32768 | tf_op jit(solution)/shard_map/all_to_all | solution.py:389
  24.3 0.0 copy-done.5
  24.3 1.6 %shard_map.103 = f32[16,24,128]{2,1,0:T(8,128)S(1)} custom-call(s32[16]{0:T(128)S(1)} %copy-done.5, f32[16,2,128]{2,1,0:T(2,128)S(1)} %all_to_all.20.stat_ref, f32[32,640]{1,0:T(8,128)S(1)} %get-tuple-element.26.sp_ref, f32[2,32,1024]{2,1,0:T(8,128)S(1)} %get-tuple-element.27.sr_ref, bf16[576,640]{1,0:T(8,128)(2,1)S(1)} %get-tuple-element.20.keys_ref, ...), custom_call_target="tpu_custom_call" | custom-call | tf_op jit(solution)/shard_map/pallas_call | solution.py:476
  26.0 0.0 copy-done.1
  26.0 0.5 collective-permute-start.1
  26.4 10.0 %all_to_all.21.part_ref = f32[16,24,128]{2,1,0:T(8,128)S(1)} all-to-all(f32[16,24,128]{2,1,0:T(8,128)S(1)} %shard_map.103), channel_id=1, replica_groups={{10,11,8,9,14,15,12,13,2,3,0,1,6,7,4,5},{26,27,24,25,30,31,28,29,18,19,..., dimensions={0} | all-to-all | bytes 393216 | tf_op jit(solution)/shard_map/all_to_all | solution.py:389
  36.4 0.0 collective-permute-done.1.other_wo_ref
  36.4 0.0 copy-done.3
  36.4 1.5 %shard_map.104 = s16[16,2,3712]{2,1,0:T(2,128)(2,1)S(1)} custom-call(s32[1,16]{1,0:T(1,128)S(1)} %bitcast.9, f32[16,24,128]{2,1,0:T(8,128)S(1)} %all_to_all.21.part_ref, bf16[1,512,128]{2,1,0:T(8,128)(2,1)S(1)} %copy-done.3, bf16[1,512,128]{2,1,0:T(8,128)(2,1)S(1)} %collective-permute-done.other_uv_ref, bf16[1,128,7168]{2,1,0:T(8,128)(2,1)S(1)} %copy-done.1, ...), custom_call_target="tpu_custom_call" | custom-call | tf_op jit(solution)/shard_map/pallas_call | solution.py:484
  38.0 11.7 %all_to_all.22.in_ref = s16[16,2,3712]{2,1,0:T(2,128)(2,1)S(1)} all-to-all(s16[16,2,3712]{2,1,0:T(2,128)(2,1)S(1)} %shard_map.104), channel_id=1, replica_groups={{10,11,8,9,14,15,12,13,2,3,0,1,6,7,4,5},{26,27,24,25,30,31,28,29,18,19,..., dimensions={0} | all-to-all | bytes 475136 | tf_op jit(solution)/shard_map/all_to_all | solution.py:389
  49.7 0.8 %shard_map.105 = bf16[1,2,7168]{2,1,0:T(2,128)(2,1)} custom-call(s16[16,2,3712]{2,1,0:T(2,128)(2,1)S(1)} %all_to_all.22.in_ref), custom_call_target="tpu_custom_call" | custom-call | tf_op jit(solution)/shard_map/pallas_call | solution.py:487
Async XLA Ops:
  2.0 12.5 %all-to-all-start = ((bf16[16,16,256]{2,1,0:T(8,128)(2,1)}), bf16[16,16,256]{2,1,0:T(8,128)(2,1)S(1)}, u32[]{:S(2)}, u32[]{:S(2)}) async-start(bf16[16,16,256]{2,1,0:T(8,128)(2,1)} %get-tuple-element.18), calls=%async_computation | async-start | bytes 262144 | tf_op jit(solution)/shard_map/all_to_all | solution.py:389
  10.1 5.8 %collective-permute-start = (bf16[1,512,128]{2,1,0:T(8,128)(2,1)}, bf16[1,512,128]{2,1,0:T(8,128)(2,1)S(1)}, u32[]{:S(2)}, u32[]{:S(2)}) collective-permute-start(bf16[1,512,128]{2,1,0:T(8,128)(2,1)} %uv_ref), channel_id=1, source_target_pairs={{0,1},{1,0},{2,3},{3,2},{4,5},{5,4},{6,7},{7,6},{8,9},{9,8},{10,11... | collective-permute-start | bytes 393224 | tf_op jit(solution)/shard_map/ppermute | solution.py:394
  10.4 1.7 %copy-start = (bf16[2,1024,576]{1,2,0:T(8,128)(2,1)S(1)}, bf16[2,1024,576]{1,2,0:T(8,128)(2,1)}, u32[]{:S(2)}) copy-start(bf16[2,1024,576]{1,2,0:T(8,128)(2,1)} %param.13) | copy-start | bytes 7077892
  12.1 1.1 %copy-start.2 = (bf16[1,512,576]{1,2,0:T(8,128)(2,1)S(1)}, bf16[1,512,576]{1,2,0:T(8,128)(2,1)}, u32[]{:S(2)}) copy-start(bf16[1,512,576]{1,2,0:T(8,128)(2,1)} %param.10) | copy-start | bytes 1769476
  13.2 0.7 %copy-start.4 = (f32[8,640]{1,0:T(8,128)S(1)}, f32[8,640]{1,0:T(8,128)}, u32[]{:S(2)}) copy-start(f32[8,640]{1,0:T(8,128)} %get-tuple-element.19.aux_ref) | copy-start | bytes 61444
  14.6 9.8 %copy-start.5 = (s32[16]{0:T(128)S(1)}, s32[16]{0:T(128)}, u32[]{:S(2)}) copy-start(s32[16]{0:T(128)} %owners_ref.1) | copy-start | bytes 196
  15.9 10.1 %copy-start.1 = (bf16[1,128,7168]{2,1,0:T(8,128)(2,1)S(1)}, bf16[1,128,7168]{2,1,0:T(8,128)(2,1)}, u32[]{:S(2)}) copy-start(bf16[1,128,7168]{2,1,0:T(8,128)(2,1)} %wo_ref) | copy-start | bytes 5505028
  15.9 20.6 %copy-start.3 = (bf16[1,512,128]{2,1,0:T(8,128)(2,1)S(1)}, bf16[1,512,128]{2,1,0:T(8,128)(2,1)}, u32[]{:S(2)}) copy-start(bf16[1,512,128]{2,1,0:T(8,128)(2,1)} %uv_ref) | copy-start | bytes 393220
  26.0 10.5 %collective-permute-start.1 = (bf16[1,128,7168]{2,1,0:T(8,128)(2,1)S(1)}, bf16[1,128,7168]{2,1,0:T(8,128)(2,1)S(1)}, u32[]{:S(2)}, u32[]{:S(2)}) collective-permute-start(bf16[1,128,7168]{2,1,0:T(8,128)(2,1)S(1)} %copy-done.1), channel_id=1, source_target_pairs={{0,1},{1,0},{2,3},{3,2},{4,5},{5,4},{6,7},{7,6},{8,9},{9,8},{10,11... | collective-permute-start | bytes 5505032 | tf_op jit(solution)/shard_map/ppermute | solution.py:394

commit v4 on v3

--- a/solution.py
+++ b/solution.py
@@ -26,8 +26,9 @@
     return lax.broadcasted_iota(I32, shape, dim)
 
 
-def shift_of(count):
-    return count // 2 + 2
+def place_of(device, count):
+    chips = count // 2
+    return (((chips // 2 + 1) - (device >> 1)) & (chips - 1)) * 2 + (device & 1)
 
 
 def over(x, n):
@@ -151,7 +152,7 @@
     slot = doubled(slots_of(owners), 5)
     count = out_ref.shape[0]
     shape = (count, 5 * rows)
-    dest = iota(shape, 0) ^ shift_of(count)
+    dest = place_of(iota(shape, 0), count)
     lane = iota(shape, 1)
     piece, seq, tok = over(lane, rows), over(rest_of(lane, rows), 2), rest_of(lane, 2)
     third = piece - 2
@@ -286,14 +287,13 @@
         second = jnp.where(mine & (seen == 1), s, second)
         seen = seen + jnp.where(mine, 1, 0)
 
-    shift = shift_of(heads)
-    mine = stat_ref[device ^ shift]
+    mine = stat_ref[place_of(device, heads)]
     place = over(iota((1, lanes), 1), rows)
     other = jnp.zeros((2, lanes), F32)
     pairs = [
-        (stat_ref[my_owner ^ shift], 1 + my_slot),
-        (stat_ref[first ^ shift], 0),
-        (stat_ref[second ^ shift], 0),
+        (stat_ref[place_of(my_owner, heads)], 1 + my_slot),
+        (stat_ref[place_of(first, heads)], 0),
+        (stat_ref[place_of(second, heads)], 0),
     ]
     for k, (theirs, segment) in enumerate(pairs):
         moved = jnp.zeros((2, lanes), F32)
@@ -328,15 +328,14 @@
     core = lax.axis_index("seq") % 2
     owners = owners_ref[...]
     row = iota((2 * rows, 1), 0)
-    shift = shift_of(count)
     other, place = over(row, rows), over(rest_of(row, rows), 2)
-    seq = place ^ shift
+    seq = place_of(place, count)
     head = jnp.where(other == 0, core, 1 - core)
     owner = column_of(owners, seq)
     slot = column_of(slots_of(owners), seq)
     shape = (2 * rows, count * each)
     first = jnp.broadcast_to(place * each + head, shape)
-    second = jnp.broadcast_to((owner ^ shift) * each + 2 + 2 * slot + head, shape)
+    second = jnp.broadcast_to(place_of(owner, count) * each + 2 + 2 * slot + head, shape)
     hits = []
     for cut in range(cuts):
         at = iota(shape, 1) - cut * PART
@@ -385,7 +384,7 @@
 
 def swap(x):
     count = lax.axis_size("seq")
-    order = [p ^ shift_of(count) for p in range(count)]
+    order = [place_of(p, count) for p in range(count)]
     return lax.all_to_all(x, "seq", split_axis=0, concat_axis=0, axis_index_groups=[order], tiled=True)
 
 

time: 50.9 us -> 51.1 us (level)
  no operation moved by 1% of the time
where the time goes in v4:
time: 51.1 us; the launch traced here: 50.6 us
  blocking collectives  30.3 us (59%)
  starting transfers between devices  8.85 us (17%)
  Pallas kernels  7.84 us (15%)
  local copies, waits for them, and re-layouts  3.47 us (7%)
    all_to_all x3, blocking collectives, swap(): lax.all_to_all(x, 'seq', split_axis=0, concat_axis=0, axis_index_groups=[...  30.3 us
    all_to_all x1, starting transfers between devices, swap(): lax.all_to_all(x, 'seq', split_axis=0, concat_axis=0, axis_index_groups=[...  8.03 us
    unnamed x12, local copies, waits for them, and re-layouts  3.47 us
    pallas_call x1, Pallas kernels, on_device(): call(functools.partial(query_kernel, res_rows), [jax.ShapeDtypeStruct((co...  2.02 us
    pallas_call x1, Pallas kernels, on_device(): call(attend_kernel, jax.ShapeDtypeStruct((heads, PART * (latent // LANES)...  1.62 us
    pallas_call x1, Pallas kernels, on_device(): call(project_kernel, jax.ShapeDtypeStruct((seqs, 2, half + LANES), I16),...  1.51 us
    pallas_call x1, Pallas kernels, on_device(): call(functools.partial(score_kernel, scale), [jax.ShapeDtypeStruct((2 * h...  1.26 us
  transfers between devices with their start and end apart: 3, of which 0 were waited for; matrix products, arithmetic and copies ran while one was open for 0% of the time, Pallas kernels for 4%

profile of v4, /device:TPU:1, one launch (start us, length us, event | category | flops | bytes accessed | tf_op | source)
XLA Modules:
  0.0 50.6 jit_solution(6416223214512107088)
XLA Ops:
  0.0 2.0 %shard_map.100 = (bf16[16,16,256]{2,1,0:T(8,128)(2,1)}, f32[8,640]{1,0:T(8,128)}) custom-call(s32[1,16]{1,0:T(1,128)} %bitcast.8, s32[1,16]{1,0:T(1,128)} %bitcast.12, bf16[16,1,2,192]{3,2,1,0:T(2,128)(2,1)} %bitcast.11, bf16[128,512]{1,0:T(8,128)(2,1)} %bitcast.10, bf16[16,2,576]{2,1,0:T(2,128)(2,1)} %new_hbm.1, bf16[512]{0:T(512)(128)(2,1)} %gain_hbm.1), custom_call_target="tpu_custom_call" | custom-call | tf_op jit(solution)/shard_map/pallas_call | solution.py:429
  2.0 8.0 %all-to-all-start = ((bf16[16,16,256]{2,1,0:T(8,128)(2,1)}), bf16[16,16,256]{2,1,0:T(8,128)(2,1)S(1)}, u32[]{:S(2)}, u32[]{:S(2)}) async-start(bf16[16,16,256]{2,1,0:T(8,128)(2,1)} %get-tuple-element.18), calls=%async_computation | async-start | bytes 262144 | tf_op jit(solution)/shard_map/all_to_all | solution.py:388
  10.1 0.4 collective-permute-start
  10.4 0.0 copy-start
  10.4 1.7 %copy-done = bf16[2,1024,576]{1,2,0:T(8,128)(2,1)S(1)} copy-done((bf16[2,1024,576]{1,2,0:T(8,128)(2,1)S(1)}, bf16[2,1024,576]{1,2,0:T(8,128)(2,1)}, u32[]{:S(2)}) %copy-start) | copy-done | bytes 2359320
  12.1 0.0 copy-start.2
  12.1 1.1 %copy-done.2 = bf16[1,512,576]{1,2,0:T(8,128)(2,1)S(1)} copy-done((bf16[1,512,576]{1,2,0:T(8,128)(2,1)S(1)}, bf16[1,512,576]{1,2,0:T(8,128)(2,1)}, u32[]{:S(2)}) %copy-start.2) | copy-done | bytes 589848
  13.2 0.0 copy-start.4
  13.2 0.7 %copy-done.4 = f32[8,640]{1,0:T(8,128)S(1)} copy-done((f32[8,640]{1,0:T(8,128)S(1)}, f32[8,640]{1,0:T(8,128)}, u32[]{:S(2)}) %copy-start.4) | copy-done | bytes 20504
  13.9 0.7 %shard_map.101 = (bf16[576,640]{1,0:T(8,128)(2,1)S(1)}, f32[8,640]{1,0:T(8,128)S(1)}, bf16[2,576,1024]{2,1,0:T(8,128)(2,1)S(1)}) custom-call(f32[8,640]{1,0:T(8,128)S(1)} %copy-done.4, bf16[1,576,512]{2,1,0:T(8,128)(2,1)S(1)} %bitcast.7, bf16[2,576,1024]{2,1,0:T(8,128)(2,1)S(1)} %bitcast.6), custom_call_target="tpu_custom_call" | custom-call | flops 10000000 | bytes 10000000 | tf_op jit(solution)/shard_map/pallas_call | solution.py:451
  14.6 0.0 copy-start.5
  14.6 0.0 all-to-all-done.q_ref
  14.6 1.3 %shard_map.102 = (f32[32,640]{1,0:T(8,128)S(1)}, f32[2,32,1024]{2,1,0:T(8,128)S(1)}, f32[16,2,128]{2,1,0:T(2,128)S(1)}) custom-call(bf16[16,16,256]{2,1,0:T(8,128)(2,1)S(1)} %all-to-all-done.q_ref, bf16[576,640]{1,0:T(8,128)(2,1)S(1)} %get-tuple-element.20.keys_ref, f32[8,640]{1,0:T(8,128)S(1)} %get-tuple-element.21.seen_ref, ...), custom_call_target="tpu_custom_call" | custom-call | tf_op jit(solution)/shard_map/pallas_call | solution.py:464
  15.8 0.0 copy-start.1
  15.9 0.0 copy-start.3
  15.9 0.0 collective-permute-done.other_uv_ref
  15.9 8.5 %all_to_all.20.stat_ref = f32[16,2,128]{2,1,0:T(2,128)S(1)} all-to-all(f32[16,2,128]{2,1,0:T(2,128)S(1)} %get-tuple-element.25), channel_id=1, replica_groups={{10,11,8,9,6,7,4,5,2,3,0,1,14,15,12,13},{26,27,24,25,22,23,20,21,18,19,..., dimensions={0} | all-to-all | bytes 32768 | tf_op jit(solution)/shard_map/all_to_all | solution.py:388
  24.4 0.0 copy-done.5
  24.4 1.6 %shard_map.103 = f32[16,24,128]{2,1,0:T(8,128)S(1)} custom-call(s32[16]{0:T(128)S(1)} %copy-done.5, f32[16,2,128]{2,1,0:T(2,128)S(1)} %all_to_all.20.stat_ref, f32[32,640]{1,0:T(8,128)S(1)} %get-tuple-element.26.sp_ref, f32[2,32,1024]{2,1,0:T(8,128)S(1)} %get-tuple-element.27.sr_ref, bf16[576,640]{1,0:T(8,128)(2,1)S(1)} %get-tuple-element.20.keys_ref, ...), custom_call_target="tpu_custom_call" | custom-call | tf_op jit(solution)/shard_map/pallas_call | solution.py:475
  26.0 0.0 copy-done.1
  26.0 0.5 collective-permute-start.1
  26.5 10.2 %all_to_all.21.part_ref = f32[16,24,128]{2,1,0:T(8,128)S(1)} all-to-all(f32[16,24,128]{2,1,0:T(8,128)S(1)} %shard_map.103), channel_id=1, replica_groups={{10,11,8,9,6,7,4,5,2,3,0,1,14,15,12,13},{26,27,24,25,22,23,20,21,18,19,..., dimensions={0} | all-to-all | bytes 393216 | tf_op jit(solution)/shard_map/all_to_all | solution.py:388
  36.7 0.0 collective-permute-done.1.other_wo_ref
  36.7 0.0 copy-done.3
  36.7 1.5 %shard_map.104 = s16[16,2,3712]{2,1,0:T(2,128)(2,1)S(1)} custom-call(s32[1,16]{1,0:T(1,128)S(1)} %bitcast.9, f32[16,24,128]{2,1,0:T(8,128)S(1)} %all_to_all.21.part_ref, bf16[1,512,128]{2,1,0:T(8,128)(2,1)S(1)} %copy-done.3, bf16[1,512,128]{2,1,0:T(8,128)(2,1)S(1)} %collective-permute-done.other_uv_ref, bf16[1,128,7168]{2,1,0:T(8,128)(2,1)S(1)} %copy-done.1, ...), custom_call_target="tpu_custom_call" | custom-call | tf_op jit(solution)/shard_map/pallas_call | solution.py:483
  38.3 11.6 %all_to_all.22.in_ref = s16[16,2,3712]{2,1,0:T(2,128)(2,1)S(1)} all-to-all(s16[16,2,3712]{2,1,0:T(2,128)(2,1)S(1)} %shard_map.104), channel_id=1, replica_groups={{10,11,8,9,6,7,4,5,2,3,0,1,14,15,12,13},{26,27,24,25,22,23,20,21,18,19,..., dimensions={0} | all-to-all | bytes 475136 | tf_op jit(solution)/shard_map/all_to_all | solution.py:388
  49.8 0.8 %shard_map.105 = bf16[1,2,7168]{2,1,0:T(2,128)(2,1)} custom-call(s16[16,2,3712]{2,1,0:T(2,128)(2,1)S(1)} %all_to_all.22.in_ref), custom_call_target="tpu_custom_call" | custom-call | tf_op jit(solution)/shard_map/pallas_call | solution.py:486
Async XLA Ops:
  2.0 12.5 %all-to-all-start = ((bf16[16,16,256]{2,1,0:T(8,128)(2,1)}), bf16[16,16,256]{2,1,0:T(8,128)(2,1)S(1)}, u32[]{:S(2)}, u32[]{:S(2)}) async-start(bf16[16,16,256]{2,1,0:T(8,128)(2,1)} %get-tuple-element.18), calls=%async_computation | async-start | bytes 262144 | tf_op jit(solution)/shard_map/all_to_all | solution.py:388
  10.1 5.8 %collective-permute-start = (bf16[1,512,128]{2,1,0:T(8,128)(2,1)}, bf16[1,512,128]{2,1,0:T(8,128)(2,1)S(1)}, u32[]{:S(2)}, u32[]{:S(2)}) collective-permute-start(bf16[1,512,128]{2,1,0:T(8,128)(2,1)} %uv_ref), channel_id=1, source_target_pairs={{0,1},{1,0},{2,3},{3,2},{4,5},{5,4},{6,7},{7,6},{8,9},{9,8},{10,11... | collective-permute-start | bytes 393224 | tf_op jit(solution)/shard_map/ppermute | solution.py:393
  10.4 1.7 %copy-start = (bf16[2,1024,576]{1,2,0:T(8,128)(2,1)S(1)}, bf16[2,1024,576]{1,2,0:T(8,128)(2,1)}, u32[]{:S(2)}) copy-start(bf16[2,1024,576]{1,2,0:T(8,128)(2,1)} %param.13) | copy-start | bytes 7077892
  12.1 1.1 %copy-start.2 = (bf16[1,512,576]{1,2,0:T(8,128)(2,1)S(1)}, bf16[1,512,576]{1,2,0:T(8,128)(2,1)}, u32[]{:S(2)}) copy-start(bf16[1,512,576]{1,2,0:T(8,128)(2,1)} %param.10) | copy-start | bytes 1769476
  13.2 0.7 %copy-start.4 = (f32[8,640]{1,0:T(8,128)S(1)}, f32[8,640]{1,0:T(8,128)}, u32[]{:S(2)}) copy-start(f32[8,640]{1,0:T(8,128)} %get-tuple-element.19.aux_ref) | copy-start | bytes 61444
  14.6 9.8 %copy-start.5 = (s32[16]{0:T(128)S(1)}, s32[16]{0:T(128)}, u32[]{:S(2)}) copy-start(s32[16]{0:T(128)} %owners_ref.1) | copy-start | bytes 196
  15.8 10.2 %copy-start.1 = (bf16[1,128,7168]{2,1,0:T(8,128)(2,1)S(1)}, bf16[1,128,7168]{2,1,0:T(8,128)(2,1)}, u32[]{:S(2)}) copy-start(bf16[1,128,7168]{2,1,0:T(8,128)(2,1)} %wo_ref) | copy-start | bytes 5505028
  15.9 20.9 %copy-start.3 = (bf16[1,512,128]{2,1,0:T(8,128)(2,1)S(1)}, bf16[1,512,128]{2,1,0:T(8,128)(2,1)}, u32[]{:S(2)}) copy-start(bf16[1,512,128]{2,1,0:T(8,128)(2,1)} %uv_ref) | copy-start | bytes 393220
  26.0 10.7 %collective-permute-start.1 = (bf16[1,128,7168]{2,1,0:T(8,128)(2,1)S(1)}, bf16[1,128,7168]{2,1,0:T(8,128)(2,1)S(1)}, u32[]{:S(2)}, u32[]{:S(2)}) collective-permute-start(bf16[1,128,7168]{2,1,0:T(8,128)(2,1)S(1)} %copy-done.1), channel_id=1, source_target_pairs={{0,1},{1,0},{2,3},{3,2},{4,5},{5,4},{6,7},{7,6},{8,9},{9,8},{10,11... | collective-permute-start | bytes 5505032 | tf_op jit(solution)/shard_map/ppermute | solution.py:393

commit v5 on v4

--- a/solution.py
+++ b/solution.py
@@ -306,16 +306,22 @@
     hit = iota((3 * rows, lanes), 1) == iota((3 * rows, lanes), 0)
     top = jnp.sum(jnp.where(hit, top, 0.0), axis=1, keepdims=True)
     total = jnp.sum(jnp.where(hit, total, 0.0), axis=1, keepdims=True)
+    result = None
     for k in range(3):
-        at = slice(k * rows, (k + 1) * rows)
         scores = sp_ref[...] if k == 0 else sr_ref[k - 1]
         keys = keys_ref[:latent, :] if k == 0 else resident_ref[k - 1, :latent, :]
-        weights = jnp.exp(scores - top[at]).astype(BF16)
-        part = dot(weights, keys, ((1,), (1,))) / total[at]
+        weights = jnp.exp(scores - top[k * rows : (k + 1) * rows]).astype(BF16)
+        zero = jnp.zeros(weights.shape, BF16)
+        blocks = [weights if j == k else zero for j in range(lanes // rows)]
+        one = dot(keys, jnp.concatenate(blocks, axis=0), ((1,), (1,)))
+        result = one if result is None else result + one
+    result = result.T[: 3 * rows] / total
+    for k in range(3):
         for h in range(heads):
             for c in range(latent // LANES):
                 at = c * PART + 2 * k
-                out_ref[h, at : at + 2, :] = part[2 * h : 2 * h + 2, c * LANES : (c + 1) * LANES]
+                line = k * rows + 2 * h
+                out_ref[h, at : at + 2, :] = result[line : line + 2, c * LANES : (c + 1) * LANES]
 
 
 def project_kernel(

time: 51.1 us -> 51.1 us (level)
  no operation moved by 1% of the time
where the time goes in v5:
time: 51.1 us; the launch traced here: 50.7 us
  blocking collectives  30.3 us (59%)
  starting transfers between devices  8.86 us (17%)
  Pallas kernels  7.9 us (15%)
  local copies, waits for them, and re-layouts  3.47 us (7%)
    all_to_all x3, blocking collectives, swap(): lax.all_to_all(x, 'seq', split_axis=0, concat_axis=0, axis_index_groups=[...  30.3 us
    all_to_all x1, starting transfers between devices, swap(): lax.all_to_all(x, 'seq', split_axis=0, concat_axis=0, axis_index_groups=[...  8.03 us
    unnamed x12, local copies, waits for them, and re-layouts  3.47 us
    pallas_call x1, Pallas kernels, on_device(): call(functools.partial(query_kernel, res_rows), [jax.ShapeDtypeStruct((co...  2.02 us
    pallas_call x1, Pallas kernels, on_device(): call(attend_kernel, jax.ShapeDtypeStruct((heads, PART * (latent // LANES)...  1.68 us
    pallas_call x1, Pallas kernels, on_device(): call(project_kernel, jax.ShapeDtypeStruct((seqs, 2, half + LANES), I16),...  1.51 us
    pallas_call x1, Pallas kernels, on_device(): call(functools.partial(score_kernel, scale), [jax.ShapeDtypeStruct((2 * h...  1.26 us
  transfers between devices with their start and end apart: 3, of which 0 were waited for; matrix products, arithmetic and copies ran while one was open for 0% of the time, Pallas kernels for 4%

profile of v5, /device:TPU:1, one launch (start us, length us, event | category | flops | bytes accessed | tf_op | source)
XLA Modules:
  0.0 50.7 jit_solution(4738362795756580134)
XLA Ops:
  0.0 2.0 %shard_map.100 = (bf16[16,16,256]{2,1,0:T(8,128)(2,1)}, f32[8,640]{1,0:T(8,128)}) custom-call(s32[1,16]{1,0:T(1,128)} %bitcast.8, s32[1,16]{1,0:T(1,128)} %bitcast.12, bf16[16,1,2,192]{3,2,1,0:T(2,128)(2,1)} %bitcast.11, bf16[128,512]{1,0:T(8,128)(2,1)} %bitcast.10, bf16[16,2,576]{2,1,0:T(2,128)(2,1)} %new_hbm.1, bf16[512]{0:T(512)(128)(2,1)} %gain_hbm.1), custom_call_target="tpu_custom_call" | custom-call | tf_op jit(solution)/shard_map/pallas_call | solution.py:435
  2.0 8.0 %all-to-all-start = ((bf16[16,16,256]{2,1,0:T(8,128)(2,1)}), bf16[16,16,256]{2,1,0:T(8,128)(2,1)S(1)}, u32[]{:S(2)}, u32[]{:S(2)}) async-start(bf16[16,16,256]{2,1,0:T(8,128)(2,1)} %get-tuple-element.18), calls=%async_computation | async-start | bytes 262144 | tf_op jit(solution)/shard_map/all_to_all | solution.py:394
  10.1 0.4 collective-permute-start
  10.4 0.0 copy-start
  10.4 1.7 %copy-done = bf16[2,1024,576]{1,2,0:T(8,128)(2,1)S(1)} copy-done((bf16[2,1024,576]{1,2,0:T(8,128)(2,1)S(1)}, bf16[2,1024,576]{1,2,0:T(8,128)(2,1)}, u32[]{:S(2)}) %copy-start) | copy-done | bytes 2359320
  12.1 0.0 copy-start.2
  12.1 1.1 %copy-done.2 = bf16[1,512,576]{1,2,0:T(8,128)(2,1)S(1)} copy-done((bf16[1,512,576]{1,2,0:T(8,128)(2,1)S(1)}, bf16[1,512,576]{1,2,0:T(8,128)(2,1)}, u32[]{:S(2)}) %copy-start.2) | copy-done | bytes 589848
  13.2 0.0 copy-start.4
  13.2 0.7 %copy-done.4 = f32[8,640]{1,0:T(8,128)S(1)} copy-done((f32[8,640]{1,0:T(8,128)S(1)}, f32[8,640]{1,0:T(8,128)}, u32[]{:S(2)}) %copy-start.4) | copy-done | bytes 20504
  13.9 0.7 %shard_map.101 = (bf16[576,640]{1,0:T(8,128)(2,1)S(1)}, f32[8,640]{1,0:T(8,128)S(1)}, bf16[2,576,1024]{2,1,0:T(8,128)(2,1)S(1)}) custom-call(f32[8,640]{1,0:T(8,128)S(1)} %copy-done.4, bf16[1,576,512]{2,1,0:T(8,128)(2,1)S(1)} %bitcast.7, bf16[2,576,1024]{2,1,0:T(8,128)(2,1)S(1)} %bitcast.6), custom_call_target="tpu_custom_call" | custom-call | flops 10000000 | bytes 10000000 | tf_op jit(solution)/shard_map/pallas_call | solution.py:457
  14.6 0.0 copy-start.5
  14.6 0.0 all-to-all-done.q_ref
  14.6 1.3 %shard_map.102 = (f32[32,640]{1,0:T(8,128)S(1)}, f32[2,32,1024]{2,1,0:T(8,128)S(1)}, f32[16,2,128]{2,1,0:T(2,128)S(1)}) custom-call(bf16[16,16,256]{2,1,0:T(8,128)(2,1)S(1)} %all-to-all-done.q_ref, bf16[576,640]{1,0:T(8,128)(2,1)S(1)} %get-tuple-element.20.keys_ref, f32[8,640]{1,0:T(8,128)S(1)} %get-tuple-element.21.seen_ref, ...), custom_call_target="tpu_custom_call" | custom-call | tf_op jit(solution)/shard_map/pallas_call | solution.py:470
  15.8 0.0 copy-start.1
  15.9 0.0 copy-start.3
  15.9 0.0 collective-permute-done.other_uv_ref
  15.9 8.5 %all_to_all.20.stat_ref = f32[16,2,128]{2,1,0:T(2,128)S(1)} all-to-all(f32[16,2,128]{2,1,0:T(2,128)S(1)} %get-tuple-element.25), channel_id=1, replica_groups={{10,11,8,9,6,7,4,5,2,3,0,1,14,15,12,13},{26,27,24,25,22,23,20,21,18,19,..., dimensions={0} | all-to-all | bytes 32768 | tf_op jit(solution)/shard_map/all_to_all | solution.py:394
  24.4 0.0 copy-done.5
  24.4 1.7 %shard_map.103 = f32[16,24,128]{2,1,0:T(8,128)S(1)} custom-call(s32[16]{0:T(128)S(1)} %copy-done.5, f32[16,2,128]{2,1,0:T(2,128)S(1)} %all_to_all.20.stat_ref, f32[32,640]{1,0:T(8,128)S(1)} %get-tuple-element.26.sp_ref, f32[2,32,1024]{2,1,0:T(8,128)S(1)} %get-tuple-element.27.sr_ref, bf16[576,640]{1,0:T(8,128)(2,1)S(1)} %get-tuple-element.20.keys_ref, ...), custom_call_target="tpu_custom_call" | custom-call | tf_op jit(solution)/shard_map/pallas_call | solution.py:481
  26.1 0.0 copy-done.1
  26.1 0.5 collective-permute-start.1
  26.6 10.2 %all_to_all.21.part_ref = f32[16,24,128]{2,1,0:T(8,128)S(1)} all-to-all(f32[16,24,128]{2,1,0:T(8,128)S(1)} %shard_map.103), channel_id=1, replica_groups={{10,11,8,9,6,7,4,5,2,3,0,1,14,15,12,13},{26,27,24,25,22,23,20,21,18,19,..., dimensions={0} | all-to-all | bytes 393216 | tf_op jit(solution)/shard_map/all_to_all | solution.py:394
  36.8 0.0 collective-permute-done.1.other_wo_ref
  36.8 0.0 copy-done.3
  36.8 1.5 %shard_map.104 = s16[16,2,3712]{2,1,0:T(2,128)(2,1)S(1)} custom-call(s32[1,16]{1,0:T(1,128)S(1)} %bitcast.9, f32[16,24,128]{2,1,0:T(8,128)S(1)} %all_to_all.21.part_ref, bf16[1,512,128]{2,1,0:T(8,128)(2,1)S(1)} %copy-done.3, bf16[1,512,128]{2,1,0:T(8,128)(2,1)S(1)} %collective-permute-done.other_uv_ref, bf16[1,128,7168]{2,1,0:T(8,128)(2,1)S(1)} %copy-done.1, ...), custom_call_target="tpu_custom_call" | custom-call | tf_op jit(solution)/shard_map/pallas_call | solution.py:489
  38.3 11.6 %all_to_all.22.in_ref = s16[16,2,3712]{2,1,0:T(2,128)(2,1)S(1)} all-to-all(s16[16,2,3712]{2,1,0:T(2,128)(2,1)S(1)} %shard_map.104), channel_id=1, replica_groups={{10,11,8,9,6,7,4,5,2,3,0,1,14,15,12,13},{26,27,24,25,22,23,20,21,18,19,..., dimensions={0} | all-to-all | bytes 475136 | tf_op jit(solution)/shard_map/all_to_all | solution.py:394
  49.9 0.8 %shard_map.105 = bf16[1,2,7168]{2,1,0:T(2,128)(2,1)} custom-call(s16[16,2,3712]{2,1,0:T(2,128)(2,1)S(1)} %all_to_all.22.in_ref), custom_call_target="tpu_custom_call" | custom-call | tf_op jit(solution)/shard_map/pallas_call | solution.py:492
Async XLA Ops:
  2.0 12.5 %all-to-all-start = ((bf16[16,16,256]{2,1,0:T(8,128)(2,1)}), bf16[16,16,256]{2,1,0:T(8,128)(2,1)S(1)}, u32[]{:S(2)}, u32[]{:S(2)}) async-start(bf16[16,16,256]{2,1,0:T(8,128)(2,1)} %get-tuple-element.18), calls=%async_computation | async-start | bytes 262144 | tf_op jit(solution)/shard_map/all_to_all | solution.py:394
  10.1 5.8 %collective-permute-start = (bf16[1,512,128]{2,1,0:T(8,128)(2,1)}, bf16[1,512,128]{2,1,0:T(8,128)(2,1)S(1)}, u32[]{:S(2)}, u32[]{:S(2)}) collective-permute-start(bf16[1,512,128]{2,1,0:T(8,128)(2,1)} %uv_ref), channel_id=1, source_target_pairs={{0,1},{1,0},{2,3},{3,2},{4,5},{5,4},{6,7},{7,6},{8,9},{9,8},{10,11... | collective-permute-start | bytes 393224 | tf_op jit(solution)/shard_map/ppermute | solution.py:399
  10.4 1.7 %copy-start = (bf16[2,1024,576]{1,2,0:T(8,128)(2,1)S(1)}, bf16[2,1024,576]{1,2,0:T(8,128)(2,1)}, u32[]{:S(2)}) copy-start(bf16[2,1024,576]{1,2,0:T(8,128)(2,1)} %param.13) | copy-start | bytes 7077892
  12.1 1.1 %copy-start.2 = (bf16[1,512,576]{1,2,0:T(8,128)(2,1)S(1)}, bf16[1,512,576]{1,2,0:T(8,128)(2,1)}, u32[]{:S(2)}) copy-start(bf16[1,512,576]{1,2,0:T(8,128)(2,1)} %param.10) | copy-start | bytes 1769476
  13.2 0.7 %copy-start.4 = (f32[8,640]{1,0:T(8,128)S(1)}, f32[8,640]{1,0:T(8,128)}, u32[]{:S(2)}) copy-start(f32[8,640]{1,0:T(8,128)} %get-tuple-element.19.aux_ref) | copy-start | bytes 61444
  14.6 9.8 %copy-start.5 = (s32[16]{0:T(128)S(1)}, s32[16]{0:T(128)}, u32[]{:S(2)}) copy-start(s32[16]{0:T(128)} %owners_ref.1) | copy-start | bytes 196
  15.8 10.2 %copy-start.1 = (bf16[1,128,7168]{2,1,0:T(8,128)(2,1)S(1)}, bf16[1,128,7168]{2,1,0:T(8,128)(2,1)}, u32[]{:S(2)}) copy-start(bf16[1,128,7168]{2,1,0:T(8,128)(2,1)} %wo_ref) | copy-start | bytes 5505028
  15.9 20.9 %copy-start.3 = (bf16[1,512,128]{2,1,0:T(8,128)(2,1)S(1)}, bf16[1,512,128]{2,1,0:T(8,128)(2,1)}, u32[]{:S(2)}) copy-start(bf16[1,512,128]{2,1,0:T(8,128)(2,1)} %uv_ref) | copy-start | bytes 393220
  26.1 10.7 %collective-permute-start.1 = (bf16[1,128,7168]{2,1,0:T(8,128)(2,1)S(1)}, bf16[1,128,7168]{2,1,0:T(8,128)(2,1)S(1)}, u32[]{:S(2)}, u32[]{:S(2)}) collective-permute-start(bf16[1,128,7168]{2,1,0:T(8,128)(2,1)S(1)} %copy-done.1), channel_id=1, source_target_pairs={{0,1},{1,0},{2,3},{3,2},{4,5},{5,4},{6,7},{7,6},{8,9},{9,8},{10,11... | collective-permute-start | bytes 5505032 | tf_op jit(solution)/shard_map/ppermute | solution.py:399

commit v6 on v4

--- a/solution.py
+++ b/solution.py
@@ -148,8 +148,8 @@
         blocks = [turned if j == k else zero for j in range(half // rope)]
         pieces.append(jnp.concatenate(blocks, axis=1).astype(BF16))
     owners = owners_ref[...]
-    owner = doubled(owners, 5)
-    slot = doubled(slots_of(owners), 5)
+    packed = doubled(owners * 4 + slots_of(owners), 5)
+    owner, slot = over(packed, 4), rest_of(packed, 4)
     count = out_ref.shape[0]
     shape = (count, 5 * rows)
     dest = place_of(iota(shape, 0), count)
@@ -266,7 +266,7 @@
 
 
 def attend_kernel(
-    owners_ref, stat_ref, sp_ref, sr_ref, keys_ref, resident_ref, out_ref
+    owners_ref, stat_ref, sp_ref, sr_ref, keys_ref, resident_ref, _, out_ref, __
 ):
     heads = out_ref.shape[0]
     latent = out_ref.shape[1] // PART * LANES
@@ -331,8 +331,8 @@
     other, place = over(row, rows), over(rest_of(row, rows), 2)
     seq = place_of(place, count)
     head = jnp.where(other == 0, core, 1 - core)
-    owner = column_of(owners, seq)
-    slot = column_of(slots_of(owners), seq)
+    packed = column_of(owners * 4 + slots_of(owners), seq)
+    owner, slot = over(packed, 4), rest_of(packed, 4)
     shape = (2 * rows, count * each)
     first = jnp.broadcast_to(place * each + head, shape)
     second = jnp.broadcast_to(place_of(owner, count) * each + 2 + 2 * slot + head, shape)
@@ -393,7 +393,7 @@
     return lax.ppermute(x, "seq", [(d, d ^ step) for d in range(count)])
 
 
-def call(kernel, shapes, specs, scratch=(), cost=None, room=None):
+def call(kernel, shapes, specs, scratch=(), cost=None, room=None, outs=None, aliases={}):
     single = not isinstance(shapes, (list, tuple))
     if room is None:
         room = 16 if lax.axis_size("seq") <= 32 else 56
@@ -401,7 +401,8 @@
         kernel,
         out_shape=shapes,
         in_specs=specs,
-        out_specs=VMEM if single else [VMEM] * len(shapes),
+        out_specs=VMEM if single else outs or [VMEM] * len(shapes),
+        input_output_aliases=aliases,
         scratch_shapes=list(scratch),
         cost_estimate=cost,
         compiler_params=pltpu.CompilerParams(vmem_limit_bytes=room * 1024 * 1024),
@@ -470,15 +471,19 @@
         ],
         [VMEM] * 4,
     )(received, keys, seen, resident)
-    stat, other_uv = lax.optimization_barrier((stat, other_uv))
+    stat, other_uv, w_o = lax.optimization_barrier((stat, other_uv, w_o))
+    other_wo = trade(w_o, 1)
     stats = swap(stat)
-    part = call(
+    part, other_wo = call(
         attend_kernel,
-        jax.ShapeDtypeStruct((heads, PART * (latent // LANES), LANES), F32),
-        [SMEM] + [VMEM] * 5,
-    )(owners, stats, scores_p, scores_r, keys, resident)
-    part, w_o = lax.optimization_barrier((part, w_o))
-    other_wo = trade(w_o, 1)
+        [
+            jax.ShapeDtypeStruct((heads, PART * (latent // LANES), LANES), F32),
+            jax.ShapeDtypeStruct(w_o.shape, BF16),
+        ],
+        [SMEM] + [VMEM] * 5 + [HBM],
+        outs=[VMEM, HBM],
+        aliases={6: 1},
+    )(owners, stats, scores_p, scores_r, keys, resident, other_wo)
     parts = swap(part)
     sums = call(
         project_kernel, jax.ShapeDtypeStruct((seqs, 2, half + LANES), I16), [VMEM] * 6

time: 51.1 us -> 51.1 us (level)
  no operation moved by 1% of the time
where the time goes in v6:
time: 51.1 us; the launch traced here: 50.6 us
  blocking collectives  30.4 us (59%)
  starting transfers between devices  8.54 us (17%)
  Pallas kernels  7.88 us (15%)
  local copies, waits for them, and re-layouts  3.69 us (7%)
    all_to_all x3, blocking collectives, swap(): lax.all_to_all(x, 'seq', split_axis=0, concat_axis=0, axis_index_groups=[...  30.4 us
    all_to_all x1, starting transfers between devices, swap(): lax.all_to_all(x, 'seq', split_axis=0, concat_axis=0, axis_index_groups=[...  8.03 us
    unnamed x12, local copies, waits for them, and re-layouts  3.69 us
    pallas_call x1, Pallas kernels, on_device(): call(functools.partial(query_kernel, res_rows), [jax.ShapeDtypeStruct((co...  2.04 us
    pallas_call x1, Pallas kernels, on_device(): call(attend_kernel, [jax.ShapeDtypeStruct((heads, PART * (latent // LANES...  1.63 us
    pallas_call x1, Pallas kernels, on_device(): call(project_kernel, jax.ShapeDtypeStruct((seqs, 2, half + LANES), I16),...  1.52 us
    pallas_call x1, Pallas kernels, on_device(): call(functools.partial(score_kernel, scale), [jax.ShapeDtypeStruct((2 * h...  1.26 us
  transfers between devices with their start and end apart: 3, of which 0 were waited for; matrix products, arithmetic and copies ran while one was open for 0% of the time, Pallas kernels for 4%

profile of v6, /device:TPU:1, one launch (start us, length us, event | category | flops | bytes accessed | tf_op | source)
XLA Modules:
  0.0 50.6 jit_solution(12247892271345019325)
XLA Ops:
  0.0 2.0 %shard_map.100 = (bf16[16,16,256]{2,1,0:T(8,128)(2,1)}, f32[8,640]{1,0:T(8,128)}) custom-call(s32[1,16]{1,0:T(1,128)} %bitcast.8, s32[1,16]{1,0:T(1,128)} %bitcast.12, bf16[16,1,2,192]{3,2,1,0:T(2,128)(2,1)} %bitcast.11, bf16[128,512]{1,0:T(8,128)(2,1)} %bitcast.10, bf16[16,2,576]{2,1,0:T(2,128)(2,1)} %new_hbm.1, bf16[512]{0:T(512)(128)(2,1)} %gain_hbm.1), custom_call_target="tpu_custom_call" | custom-call | tf_op jit(solution)/shard_map/pallas_call | solution.py:430
  2.0 8.0 %all-to-all-start = ((bf16[16,16,256]{2,1,0:T(8,128)(2,1)}), bf16[16,16,256]{2,1,0:T(8,128)(2,1)S(1)}, u32[]{:S(2)}, u32[]{:S(2)}) async-start(bf16[16,16,256]{2,1,0:T(8,128)(2,1)} %get-tuple-element.19), calls=%async_computation | async-start | bytes 262144 | tf_op jit(solution)/shard_map/all_to_all | solution.py:388
  10.1 0.4 collective-permute-start
  10.4 0.0 copy-start
  10.4 1.7 %copy-done = bf16[2,1024,576]{1,2,0:T(8,128)(2,1)S(1)} copy-done((bf16[2,1024,576]{1,2,0:T(8,128)(2,1)S(1)}, bf16[2,1024,576]{1,2,0:T(8,128)(2,1)}, u32[]{:S(2)}) %copy-start) | copy-done | bytes 2359320
  12.1 0.0 copy-start.2
  12.1 1.1 %copy-done.2 = bf16[1,512,576]{1,2,0:T(8,128)(2,1)S(1)} copy-done((bf16[1,512,576]{1,2,0:T(8,128)(2,1)S(1)}, bf16[1,512,576]{1,2,0:T(8,128)(2,1)}, u32[]{:S(2)}) %copy-start.2) | copy-done | bytes 589848
  13.2 0.0 copy-start.4
  13.2 0.7 %copy-done.4 = f32[8,640]{1,0:T(8,128)S(1)} copy-done((f32[8,640]{1,0:T(8,128)S(1)}, f32[8,640]{1,0:T(8,128)}, u32[]{:S(2)}) %copy-start.4) | copy-done | bytes 20504
  13.9 0.7 %shard_map.101 = (bf16[576,640]{1,0:T(8,128)(2,1)S(1)}, f32[8,640]{1,0:T(8,128)S(1)}, bf16[2,576,1024]{2,1,0:T(8,128)(2,1)S(1)}) custom-call(f32[8,640]{1,0:T(8,128)S(1)} %copy-done.4, bf16[1,576,512]{2,1,0:T(8,128)(2,1)S(1)} %bitcast.7, bf16[2,576,1024]{2,1,0:T(8,128)(2,1)S(1)} %bitcast.6), custom_call_target="tpu_custom_call" | custom-call | flops 10000000 | bytes 10000000 | tf_op jit(solution)/shard_map/pallas_call | solution.py:452
  14.6 0.0 copy-start.5
  14.6 0.0 all-to-all-done.q_ref
  14.6 0.0 copy-start.1
  14.6 1.3 %shard_map.102 = (f32[32,640]{1,0:T(8,128)S(1)}, f32[2,32,1024]{2,1,0:T(8,128)S(1)}, f32[16,2,128]{2,1,0:T(2,128)S(1)}) custom-call(bf16[16,16,256]{2,1,0:T(8,128)(2,1)S(1)} %all-to-all-done.q_ref, bf16[576,640]{1,0:T(8,128)(2,1)S(1)} %get-tuple-element.21.keys_ref, f32[8,640]{1,0:T(8,128)S(1)} %get-tuple-element.22.seen_ref, ...), custom_call_target="tpu_custom_call" | custom-call | tf_op jit(solution)/shard_map/pallas_call | solution.py:465
  15.9 0.0 collective-permute-done.other_uv_ref
  15.9 0.2 copy-done.1
  16.1 0.1 collective-permute-start.1
  16.3 8.3 %all_to_all.20.stat_ref = f32[16,2,128]{2,1,0:T(2,128)S(1)} all-to-all(f32[16,2,128]{2,1,0:T(2,128)S(1)} %get-tuple-element.26), channel_id=1, replica_groups={{10,11,8,9,6,7,4,5,2,3,0,1,14,15,12,13},{26,27,24,25,22,23,20,21,18,19,..., dimensions={0} | all-to-all | bytes 32768 | tf_op jit(solution)/shard_map/all_to_all | solution.py:388
  24.6 0.0 collective-permute-done.1._
  24.6 0.0 copy-done.5
  24.6 0.0 copy-start.3
  24.6 1.6 %shard_map.103 = (f32[16,24,128]{2,1,0:T(8,128)S(1)}, bf16[1,128,7168]{2,1,0:T(8,128)(2,1)S(1)}) custom-call(s32[16]{0:T(128)S(1)} %copy-done.5, f32[16,2,128]{2,1,0:T(2,128)S(1)} %all_to_all.20.stat_ref, f32[32,640]{1,0:T(8,128)S(1)} %get-tuple-element.27.sp_ref, f32[2,32,1024]{2,1,0:T(8,128)S(1)} %get-tuple-element.28.sr_ref, ...), custom_call_target="tpu_custom_call", output_to_operand_aliasing={{1}: (6, {})} | custom-call | tf_op jit(solution)/shard_map/pallas_call | solution.py:477
  26.2 10.5 %all_to_all.21.part_ref = f32[16,24,128]{2,1,0:T(8,128)S(1)} all-to-all(f32[16,24,128]{2,1,0:T(8,128)S(1)} %get-tuple-element.30), channel_id=1, replica_groups={{10,11,8,9,6,7,4,5,2,3,0,1,14,15,12,13},{26,27,24,25,22,23,20,21,18,19,..., dimensions={0} | all-to-all | bytes 393216 | tf_op jit(solution)/shard_map/all_to_all | solution.py:388
  36.8 0.0 copy-done.3
  36.8 1.5 %shard_map.104 = s16[16,2,3712]{2,1,0:T(2,128)(2,1)S(1)} custom-call(s32[1,16]{1,0:T(1,128)S(1)} %bitcast.9, f32[16,24,128]{2,1,0:T(8,128)S(1)} %all_to_all.21.part_ref, bf16[1,512,128]{2,1,0:T(8,128)(2,1)S(1)} %copy-done.3, bf16[1,512,128]{2,1,0:T(8,128)(2,1)S(1)} %collective-permute-done.other_uv_ref, bf16[1,128,7168]{2,1,0:T(8,128)(2,1)S(1)} %copy-done.1, ...), custom_call_target="tpu_custom_call" | custom-call | tf_op jit(solution)/shard_map/pallas_call | solution.py:488
  38.3 11.6 %all_to_all.22.in_ref = s16[16,2,3712]{2,1,0:T(2,128)(2,1)S(1)} all-to-all(s16[16,2,3712]{2,1,0:T(2,128)(2,1)S(1)} %shard_map.104), channel_id=1, replica_groups={{10,11,8,9,6,7,4,5,2,3,0,1,14,15,12,13},{26,27,24,25,22,23,20,21,18,19,..., dimensions={0} | all-to-all | bytes 475136 | tf_op jit(solution)/shard_map/all_to_all | solution.py:388
  49.9 0.8 %shard_map.105 = bf16[1,2,7168]{2,1,0:T(2,128)(2,1)} custom-call(s16[16,2,3712]{2,1,0:T(2,128)(2,1)S(1)} %all_to_all.22.in_ref), custom_call_target="tpu_custom_call" | custom-call | tf_op jit(solution)/shard_map/pallas_call | solution.py:491
Async XLA Ops:
  2.0 12.5 %all-to-all-start = ((bf16[16,16,256]{2,1,0:T(8,128)(2,1)}), bf16[16,16,256]{2,1,0:T(8,128)(2,1)S(1)}, u32[]{:S(2)}, u32[]{:S(2)}) async-start(bf16[16,16,256]{2,1,0:T(8,128)(2,1)} %get-tuple-element.19), calls=%async_computation | async-start | bytes 262144 | tf_op jit(solution)/shard_map/all_to_all | solution.py:388
  10.1 5.8 %collective-permute-start = (bf16[1,512,128]{2,1,0:T(8,128)(2,1)}, bf16[1,512,128]{2,1,0:T(8,128)(2,1)S(1)}, u32[]{:S(2)}, u32[]{:S(2)}) collective-permute-start(bf16[1,512,128]{2,1,0:T(8,128)(2,1)} %uv_ref), channel_id=1, source_target_pairs={{0,1},{1,0},{2,3},{3,2},{4,5},{5,4},{6,7},{7,6},{8,9},{9,8},{10,11... | collective-permute-start | bytes 393224 | tf_op jit(solution)/shard_map/ppermute | solution.py:393
  10.4 1.7 %copy-start = (bf16[2,1024,576]{1,2,0:T(8,128)(2,1)S(1)}, bf16[2,1024,576]{1,2,0:T(8,128)(2,1)}, u32[]{:S(2)}) copy-start(bf16[2,1024,576]{1,2,0:T(8,128)(2,1)} %param.13) | copy-start | bytes 7077892
  12.1 1.1 %copy-start.2 = (bf16[1,512,576]{1,2,0:T(8,128)(2,1)S(1)}, bf16[1,512,576]{1,2,0:T(8,128)(2,1)}, u32[]{:S(2)}) copy-start(bf16[1,512,576]{1,2,0:T(8,128)(2,1)} %param.10) | copy-start | bytes 1769476
  13.2 0.7 %copy-start.4 = (f32[8,640]{1,0:T(8,128)S(1)}, f32[8,640]{1,0:T(8,128)}, u32[]{:S(2)}) copy-start(f32[8,640]{1,0:T(8,128)} %get-tuple-element.20.aux_ref) | copy-start | bytes 61444
  14.6 10.0 %copy-start.5 = (s32[16]{0:T(128)S(1)}, s32[16]{0:T(128)}, u32[]{:S(2)}) copy-start(s32[16]{0:T(128)} %owners_ref.1) | copy-start | bytes 196
  14.6 1.5 %copy-start.1 = (bf16[1,128,7168]{2,1,0:T(8,128)(2,1)S(1)}, bf16[1,128,7168]{2,1,0:T(8,128)(2,1)}, u32[]{:S(2)}) copy-start(bf16[1,128,7168]{2,1,0:T(8,128)(2,1)} %wo_ref) | copy-start | bytes 5505028
  16.1 8.5 %collective-permute-start.1 = (bf16[1,128,7168]{2,1,0:T(8,128)(2,1)S(1)}, bf16[1,128,7168]{2,1,0:T(8,128)(2,1)S(1)}, u32[]{:S(2)}, u32[]{:S(2)}) collective-permute-start(bf16[1,128,7168]{2,1,0:T(8,128)(2,1)S(1)} %copy-done.1), channel_id=1, source_target_pairs={{0,1},{1,0},{2,3},{3,2},{4,5},{5,4},{6,7},{7,6},{8,9},{9,8},{10,11... | collective-permute-start | bytes 5505032 | tf_op jit(solution)/shard_map/ppermute | solution.py:393
  24.6 12.2 %copy-start.3 = (bf16[1,512,128]{2,1,0:T(8,128)(2,1)S(1)}, bf16[1,512,128]{2,1,0:T(8,128)(2,1)}, u32[]{:S(2)}) copy-start(bf16[1,512,128]{2,1,0:T(8,128)(2,1)} %uv_ref) | copy-start | bytes 393220
